TPU v7x, 128 devices: a whole 4x4x4 slice. The times are simulated.
128 devices in a mesh: row: 8 (over y_lo, x), key: 16 (over z, y_hi, core).
Axes of the slice: x: 4, y: 4 (y_hi: 2, y_lo: 2; y = y_hi * 2 + y_lo), z: 4, core: 2. Of those that a mesh axis runs over, the one named last changes fastest.
Arguments:
- pair_window: bfloat16 [8, 4096, 128], P('row', 'key'), may hold values from -30 to 30
- ln_gain: float32 [128], replicated, may hold values from 0.1 to 1.9
- w_proj: bfloat16 [128, 512], replicated, may hold values from -0.5 to 0.5
- w_out: bfloat16 [128, 128], replicated, may hold values from -0.5 to 0.5
- pair_bias: bfloat16 [4, 4096, 4096], P(None, 'row', 'key'), may hold values from -10 to 330
- chain_starts: int32 [4], replicated, may hold values from 0 to 3072, as said below
- chain_pads: int32 [4], replicated, may hold values from 0 to 256, as said below
- residue_mask: int32 [4096], replicated, may hold values 0 or 1
Outputs:
- mixed: bfloat16 [8, 4096, 128], P('row', 'key')
Inputs may be any that keep to these rules, and one draw needn't show every extreme that they name: `chain_starts`: strictly rising; the first is 0 and the last is 3072; the second and third lie 4096 // 8 to 1024 beyond the one before. `chain_pads`: some chain has exactly 256 padded positions.
All inputs are finite; a program needn't handle non-finite values.
Results may differ from a plain program's by a relative error of at most 0.0054.
The roundings to bfloat16 on the way count: a program that leaves them out, or rounds other values in their place, can miss the bound.
Values may be sent and summed in bfloat16 or wider, within the bound.
A program may use at most 192 MiB of HBM per device.

v0:
```python
import jax
import jax.numpy as jnp
from jax import lax
from jax.sharding import PartitionSpec as P

HEADS = 4
KEYBLK = 128


epsilon = 1e-05
dead_score = -1000000000.0


def merged_2(value, axis, join):
    pieces = jax.tree.map(lambda part: lax.all_gather(part, axis), value)
    head = jax.tree.map(lambda part: part[0], pieces)
    tail = jax.tree.map(lambda part: part[1:], pieces)
    running, _ = lax.scan(lambda running, share: (join(running, share), None), head, tail)
    return running


def key_alive(chain_starts, chain_pads, residue_mask, length):
    places = jnp.arange(length, dtype=jnp.int32)
    chain_ends = jnp.concatenate([chain_starts[1:], jnp.full((1,), length, jnp.int32)]) - chain_pads
    inside = (places[:, None] >= chain_starts[None, :]) & (places[:, None] < chain_ends[None, :])
    leading = places[:, None] == chain_starts[None, :]
    return jnp.any(inside, axis=1) & ((residue_mask == 1) | jnp.any(leading, axis=1))


def project(pair_rows, ln_gain, w_proj):
    channels = pair_rows.shape[-1]
    head_width = channels // HEADS
    values = pair_rows.astype(jnp.float32)
    average = jnp.mean(values, axis=-1, keepdims=True)
    centred = values - average
    variance = jnp.mean(centred * centred, axis=-1, keepdims=True)
    normed = (centred * lax.rsqrt(variance + epsilon) * ln_gain).astype(jnp.bfloat16)
    flat_rows = normed.reshape(-1, channels)
    projected = jnp.dot(flat_rows, w_proj, preferred_element_type=jnp.float32)
    factors = jnp.concatenate(
        [
            jnp.full((channels,), head_width ** (-0.5), jnp.float32),
            jnp.ones((3 * channels,), jnp.float32),
        ]
    )
    return (
        (projected * factors).astype(jnp.bfloat16).reshape(pair_rows.shape[:-1] + (4 * channels,))
    )


def local_partial(query_rows, key_rows, value_rows, bias_rows, alive_keys):
    length, channels = query_rows.shape
    key_count = key_rows.shape[0]
    head_width = channels // HEADS
    blocks = key_count // KEYBLK
    live_blocks = alive_keys.reshape(blocks, KEYBLK)
    maxima = []
    totals = []
    accums = []
    for head_index in range(HEADS):
        low_col = head_index * head_width
        high_col = low_col + head_width
        scores = lax.dot_general(
            query_rows[:, low_col:high_col],
            key_rows[:, low_col:high_col],
            (((1,), (1,)), ((), ())),
            preferred_element_type=jnp.float32,
        )
        scores = (scores + bias_rows[head_index].astype(jnp.float32)).reshape(
            length, blocks, KEYBLK
        )
        masked = jnp.where(live_blocks, scores, dead_score)
        block_max = jnp.max(masked, axis=-1)
        weights = jnp.where(live_blocks, jnp.exp(masked - block_max[..., None]), 0.0)
        block_sum = jnp.sum(weights, axis=-1)
        block_acc = jnp.einsum(
            "poh,ohs->pos",
            weights.astype(jnp.bfloat16),
            value_rows[:, low_col:high_col].reshape(blocks, KEYBLK, head_width),
            preferred_element_type=jnp.float32,
        )
        local_max = jnp.max(block_max, axis=-1)
        factor = jnp.exp(block_max - local_max[:, None])
        maxima.append(local_max)
        totals.append(jnp.sum(factor * block_sum, axis=-1))
        accums.append(jnp.sum(factor[..., None] * block_acc, axis=1))
    return (
        jnp.stack(maxima, axis=-1),
        jnp.stack(totals, axis=-1),
        jnp.concatenate(accums, axis=-1),
    )


def rescale(accums, factor):
    target = accums.shape[:-1] + (HEADS, accums.shape[-1] // HEADS)
    return (accums.reshape(target) * factor[..., None]).reshape(accums.shape)


def combine_partials(first, second):
    first_max, first_total, first_acc = first
    second_max, second_total, second_acc = second
    highest = jnp.maximum(first_max, second_max)
    first_scale = jnp.exp(first_max - highest)
    second_scale = jnp.exp(second_max - highest)
    merged_acc = rescale(first_acc, first_scale) + rescale(second_acc, second_scale)
    return (highest, first_total * first_scale + second_total * second_scale, merged_acc)


def local(pair_window, ln_gain, w_proj, w_out, pair_bias, chain_starts, chain_pads, residue_mask):
    row_count, key_count, channels = pair_window.shape
    total_keys = key_count * lax.axis_size("key")
    offset = lax.axis_index("key") * key_count
    alive_all = key_alive(chain_starts, chain_pads, residue_mask, total_keys)
    alive_keys = lax.dynamic_slice_in_dim(alive_all, offset, key_count)
    projected = project(pair_window, ln_gain, w_proj)
    gathered = lax.all_gather(projected[:, :, :channels], "key", axis=1, tiled=True)
    bias_rows = lax.all_gather(pair_bias, "row", axis=1, tiled=True)

    def partial_row(row_items):
        query_rows, key_rows, value_rows = row_items
        return local_partial(query_rows, key_rows, value_rows, bias_rows, alive_keys)

    maxima, totals, accums = lax.map(
        partial_row,
        (
            gathered,
            projected[:, :, channels : 2 * channels],
            projected[:, :, 2 * channels : 3 * channels],
        ),
    )
    merged = merged_2((maxima, totals, accums), "key", combine_partials)
    totals = lax.dynamic_slice_in_dim(merged[1], offset, key_count, 1)
    accums = lax.dynamic_slice_in_dim(merged[2], offset, key_count, 1)
    target = accums.shape[:-1] + (HEADS, channels // HEADS)
    attended = (accums.reshape(target) / totals[..., None]).reshape(accums.shape)
    gate_rows = jax.nn.sigmoid(projected[:, :, 3 * channels :].astype(jnp.float32))
    gated_rows = (gate_rows * attended).astype(jnp.bfloat16)
    mixed = jnp.dot(gated_rows.reshape(-1, channels), w_out, preferred_element_type=jnp.float32)
    return mixed.astype(jnp.bfloat16).reshape(row_count, key_count, channels)


def solution(mesh):
    in_specs = (P("row", "key", None), P(), P(), P(), P(None, "row", "key"), P(), P(), P())
    out_specs = P("row", "key", None)
    return jax.shard_map(local, mesh=mesh, in_specs=in_specs, out_specs=out_specs, check_vma=False)
```

profile of v0, /device:TPU:0, one launch (start us, length us, event | category | flops | bytes accessed | tf_op | source)
XLA Modules:
  0.0 674.0 jit_solution(6215937931384669567)
XLA Ops:
  11.2 2.4 copy.57
  14.8 43.9 %all-gather.9.cloned.1.call-done = bf16[1,4096,128]{2,1,0:T(8,128)(2,1)} async-done(((bf16[1,256,128]{2,1,0:T(8,128)(2,1)}), bf16[1,4096,128]{2,1,0:T(8,128)(2,1)}) %all-gather.9.cloned.1.call-update) | async-done | bytes 1048592 | tf_op jit(solution)/shard_map/all_gather | solution.py:116
  58.8 92.2 %all-gather.11.cloned.1.call-done = bf16[4,4096,256]{1,2,0:T(8,128)(2,1)} async-done(((bf16[4,512,256]{1,2,0:T(8,128)(2,1)}), bf16[4,4096,256]{1,2,0:T(8,128)(2,1)}) %all-gather.11.cloned.1.call-update) | async-done | bytes 8388624 | tf_op jit(solution)/shard_map/all_gather | solution.py:117
  150.9 4.6 convolution_add_fusion
  155.6 5.7 copy.61
  161.2 4.4 convolution_add_fusion.1
  165.6 5.6 copy.60
  171.2 2.5 convolution_add_fusion.2
  174.0 7.8 %select_reduce_fusion.3 = (f32[4096]{0:T(1024)S(1)}, f32[4096]{0:T(1024)S(1)}, f32[4096]{0:T(1024)S(1)}, f32[4096]{0:T(1024)S(1)}, f32[4096,256]{0,1:T(8,128)}) fusion(pred[256]{0:T(512)(128)(4,1)S(1)} %dynamic-slice_and_fusion, f32[4096,256]{0,1:T(8,128)S(1)} %convolution_add_fusion.2, f32[4096,256]{0,1:T(8,128)} %convolution_add_fusion.1, ...), kind=kOutput, calls=%fused_computation.31 | convolution fusion | flops 77578240 | bytes 20054272 | tf_op jit(solution)/shard_map/while/body/eval_jaxpr/dot_general | solution.py:63
  181.8 5.6 copy.58
  187.4 5.6 copy.59
  193.8 3.5 select_reduce_fusion.7
  197.4 9.9 %fusion.10 = (f32[4096,2]{0,1:T(2,128)S(1)}, f32[4096,2]{0,1:T(2,128)S(1)}, f32[4096,2]{0,1:T(2,128)S(1)}, f32[4096,2]{0,1:T(2,128)S(1)}) fusion(f32[4096,2,128]{2,0,1:T(8,128)} %copy.58, f32[4096,2]{0,1:T(2,128)S(1)} %select_reduce_fusion.7, pred[2,128]{1,0:T(4,128)(4,1)S(1)} %bitcast.158, f32[4096,2,128]{2,0,1:T(8,128)} %copy.59, ...), kind=kLoop, calls=%fused_computation.37 | loop fusion | flops 10452992 | bytes 16941312 | tf_op jit(solution)/shard_map/while/body/eval_jaxpr/reduce_sum | solution.py:75
  207.3 7.4 %fusion.12 = (f32[4096,2]{0,1:T(2,128)S(1)}, f32[4096,2]{0,1:T(2,128)S(1)}, f32[4096,2]{0,1:T(2,128)S(1)}) fusion(f32[4096,2,128]{2,0,1:T(8,128)S(1)} %copy-done.6, f32[4096,2]{0,1:T(2,128)S(1)} %get-tuple-element.94, pred[2,128]{1,0:T(4,128)(4,1)S(1)} %bitcast.159, f32[4096,2]{0,1:T(2,128)S(1)} %get-tuple-element.95, f32[4096,2,128]{2,0,1:T(8,128)S(1)} %copy-done.4, ...), kind=kLoop, calls=%fused_computation.39 | loop fusion | flops 12558336 | bytes 12779776 | tf_op jit(solution)/shard_map/while/body/eval_jaxpr/reduce_sum | solution.py:75
  215.8 3.6 fusion.37
  219.5 2.3 fusion.40
  221.8 2.3 fusion.43
  224.1 2.3 fusion.46
  227.9 9.8 %all-gather.13.cloned.1.call-done = f32[65536,4]{0,1:T(4,128)} async-done(((f32[4096,4]{0,1:T(4,128)}), f32[65536,4]{0,1:T(4,128)}) %all-gather.13.cloned.1.call-update) | async-done | bytes 1048592 | tf_op jit(solution)/shard_map/all_gather | solution.py:15
  237.8 46.0 %all-gather.15.cloned.1.call-done = f32[65536,4]{0,1:T(4,128)} async-done(((f32[4096,4]{0,1:T(4,128)}), f32[65536,4]{0,1:T(4,128)}) %all-gather.15.cloned.1.call-update) | async-done | bytes 1048592 | tf_op jit(solution)/shard_map/all_gather | solution.py:15
  283.8 2.2 slice.154
  287.7 183.3 %all-gather.17.cloned.1.call-done = f32[65536,128]{0,1:T(8,128)} async-done(((f32[4096,128]{0,1:T(8,128)}), f32[65536,128]{0,1:T(8,128)}) %all-gather.17.cloned.1.call-update) | async-done | bytes 33554448 | tf_op jit(solution)/shard_map/all_gather | solution.py:15
  471.0 21.4 %slice.155 = f32[61440,128]{0,1:T(8,128)} slice(f32[65536,128]{0,1:T(8,128)} %all-gather.17.cloned.1.call-done), slice={[4096:65536], [0:128]} | slice | bytes 62914560 | tf_op jit(solution)/shard_map/slice | solution.py:17
  492.4 30.8 %copy.66 = f32[61440,128]{1,0:T(8,128)} copy(f32[61440,128]{0,1:T(8,128)} %slice.155) | data formatting | bytes 62914560 | tf_op jit(solution)/shard_map/slice | solution.py:17
  523.2 3.2 slice_bitcast_fusion
  526.3 137.4 %while.2 = (s32[]{:T(128)}, f32[1,4096,4]{1,2,0:T(4,128)S(1)}, f32[1,4096,4]{1,2,0:T(4,128)S(1)}, f32[1,4096,128]{1,2,0:T(8,128)}, f32[15,1,4096,4]{2,3,1,0:T(4,...) while((s32[]{:T(128)}, f32[1,4096,4]{1,2,0:T(4,128)S(1)}, ...), condition=%wide.region_25.26_spmd, body=%wide.region_24.25_spmd.sunk | while | flops 1687554 | bytes 15663209 | solution.py:18
  527.3 3.1 constant_dynamic-slice_fusion.2
  530.4 1.9 copy.76
  532.3 3.2 fusion.96
  536.5 3.1 constant_dynamic-slice_fusion.2
  539.6 1.9 copy.76
  541.5 3.2 fusion.96
  545.6 3.1 constant_dynamic-slice_fusion.2
  548.7 1.9 copy.76
  550.6 3.2 fusion.96
  554.8 3.1 constant_dynamic-slice_fusion.2
  557.9 1.9 copy.76
  559.8 3.2 fusion.96
  564.0 3.1 constant_dynamic-slice_fusion.2
  567.0 1.9 copy.76
  569.0 3.2 fusion.96
  573.1 3.1 constant_dynamic-slice_fusion.2
  576.2 1.9 copy.76
  578.1 3.2 fusion.96
  582.3 3.1 constant_dynamic-slice_fusion.2
  585.4 1.9 copy.76
  587.3 3.2 fusion.96
  591.4 3.1 constant_dynamic-slice_fusion.2
  594.5 1.9 copy.76
  596.4 3.2 fusion.96
  600.6 3.1 constant_dynamic-slice_fusion.2
  605.6 3.2 fusion.96
  609.8 3.1 constant_dynamic-slice_fusion.2
  614.8 3.2 fusion.96
  618.9 3.1 constant_dynamic-slice_fusion.2
  623.9 3.2 fusion.96
  628.1 3.1 constant_dynamic-slice_fusion.2
  633.1 3.2 fusion.96
  637.2 3.1 constant_dynamic-slice_fusion.2
  642.2 3.2 fusion.96
  646.4 3.1 constant_dynamic-slice_fusion.2
  651.4 3.2 fusion.96
  655.6 3.1 constant_dynamic-slice_fusion.2
  660.6 3.2 fusion.96
  (117 shorter events, 42.8 us)
Async XLA Ops:
  6.5 2.0 copy-start
  6.5 7.1 %copy-start.12 = (s32[4]{0:T(128)S(1)}, s32[4]{0:T(128)}, u32[]{:S(2)}) copy-start(s32[4]{0:T(128)} %param.15) | copy-start | bytes 52
  6.5 7.2 %copy-start.13 = (s32[4]{0:T(128)S(1)}, s32[4]{0:T(128)}, u32[]{:S(2)}) copy-start(s32[4]{0:T(128)} %param.16) | copy-start | bytes 52
  6.5 52.2 %all-gather.9.cloned.1.call-start = ((), (), s32[]{:S(2)}) async-start(), calls=%async_computation | async-start | bytes 1114112 | tf_op jit(solution)/shard_map/all_gather | solution.py:116
  9.7 0.7 copy-start.11
  11.1 139.8 %all-gather.11.cloned.1.call-start = ((), (), s32[]{:S(2)}) async-start(), calls=%async_computation.1 | async-start | bytes 9437184 | tf_op jit(solution)/shard_map/all_gather | solution.py:117
  13.6 224.2 %all-gather.13.cloned.1.call-start = ((), (), s32[]{:S(2)}) async-start(), calls=%async_computation.2 | async-start | bytes 1114112 | tf_op jit(solution)/shard_map/all_gather | solution.py:15
  155.6 5.7 copy-start.10
  171.2 2.8 copy-start.9
  174.0 7.8 %copy-start.8 = (f32[4096,256]{0,1:T(8,128)}, f32[4096,256]{0,1:T(8,128)S(1)}, u32[]{:S(2)}) copy-start(f32[4096,256]{0,1:T(8,128)S(1)} %convolution_add_fusion.2) | copy-start | bytes 12582916
  193.8 90.0 %all-gather.15.cloned.1.call-start = ((), (), s32[]{:S(2)}) async-start(), calls=%async_computation.3 | async-start | bytes 1114112 | tf_op jit(solution)/shard_map/all_gather | solution.py:15
  193.8 3.5 copy-start.2
  197.3 9.9 %copy-start.4 = (f32[4096,2,128]{2,0,1:T(8,128)S(1)}, f32[4096,2,128]{2,0,1:T(8,128)}, u32[]{:S(2)}) copy-start(f32[4096,2,128]{2,0,1:T(8,128)} %copy.60) | copy-start | bytes 12582916
  197.4 9.9 %copy-start.6 = (f32[4096,2,128]{2,0,1:T(8,128)S(1)}, f32[4096,2,128]{2,0,1:T(8,128)}, u32[]{:S(2)}) copy-start(f32[4096,2,128]{2,0,1:T(8,128)} %copy.59) | copy-start | bytes 12582916
  215.6 255.4 %all-gather.17.cloned.1.call-start = ((), (), s32[]{:S(2)}) async-start(), calls=%async_computation.4 | async-start | bytes 35651584 | tf_op jit(solution)/shard_map/all_gather | solution.py:15
  215.8 3.7 copy-start.7
  219.5 2.3 copy-start.5
  221.8 2.3 copy-start.3
  523.2 3.2 slice-start
  663.8 2.0 copy-start.14
  663.8 3.7 copy-start.1
Sparse Core Ops, SparseCore 0:
  11.3 47.4 all-gather.8
  60.4 90.4 all-gather.10
  193.9 43.8 all-gather.12
  240.1 43.6 all-gather.14
  286.1 184.8 all-gather.16
where the time goes:
time: 679 us; the launch traced here: 674 us
  waiting for transfers between devices  375 us (55%)
  local copies, waits for them, and re-layouts  163 us (24%)
  other arithmetic  89 us (13%)
  matrix products  32.6 us (5%)
  between operations  13.4 us (2%)
    all_gather x3, waiting for transfers between devices, merged_2(): pieces = jax.tree.map(lambda part: lax.all_gather(part, axis), value)  239 us
    all_gather x1, waiting for transfers between devices, local(): bias_rows = lax.all_gather(pair_bias, 'row', axis=1, tiled=True)  92.2 us
    dynamic_slice x30, local copies, waits for them, and re-layouts, merged_2(): lax.scan(lambda running, share: (join(running, share), None), head, tail)  75 us
    slice x5, local copies, waits for them, and re-layouts, merged_2(): tail = jax.tree.map(lambda part: part[1:], pieces)  54.4 us
    add x15, other arithmetic, combine_partials(): rescale(first_acc, first_scale) + rescale(second_acc, second_scale)  47.8 us
    all_gather x1, waiting for transfers between devices, local(): lax.all_gather(projected[:, :, :channels], 'key', axis=1, tiled=True)  43.9 us
    reshape x4, local copies, waits for them, and re-layouts, local_partial(): (scores + bias_rows[head_index].astype(jnp.float32)).reshape(length, bloc...  22.5 us
    dot_general x4, matrix products, local_partial(): lax.dot_general(query_rows[:, low_col:high_col], key_rows[:, low_col:high...  19.3 us
  transfers between devices with their start and end apart: 5, of which 5 were waited for; matrix products, arithmetic and copies ran while one was open for 6% of the time, Pallas kernels for 0%

commit v1 on v0

v1 whole, which is shorter than its diff:
```python
import functools

import jax
import jax.numpy as jnp
from jax import lax
from jax.experimental import pallas as pl
from jax.experimental.pallas import tpu as pltpu
from jax.sharding import PartitionSpec as P

HEADS = 4
KEYBLK = 128
WIDTH = 32
CH = 128
CHUNK = 256
NX, NYL, NZ, NYH = 4, 2, 4, 2
NR = NX * NYL
NM = NZ * NYH
STAT = HEADS * WIDTH
MSG = STAT + 2 * HEADS
MESH = pl.DeviceIdType.MESH
F32 = jnp.float32
BF16 = jnp.bfloat16

epsilon = 1e-05
dead_score = -1000000000.0
dead_bias = -1e30


def contract(a, b, dim_a, dim_b):
    return lax.dot_general(a, b, (((dim_a,), (dim_b,)), ((), ())), preferred_element_type=F32)


def shifts():
    return [(a, b) for b in range(NYL) for a in range(NX) if (a, b) != (0, 0)]


def kernel(
    starts_ref, pads_ref, x_ref, gain_ref, wqT_ref, wk_ref, wvT_ref, wgT_ref, w_out_ref, mask_ref, bias_ref, out_ref,
    nbuf, qbuf, braw, biasT, own, sbuf, rbuf,
    kv_ss, kv_rs, sib_ss, sib_rs, q_ss, q_rs, t_ss, bias_ss, bias_rs, bias_ls, home_ss, home_rs, home_ls,
):
    r = lax.axis_index("row")
    c = lax.axis_index("key")
    m = c // 2
    e = c % 2
    x, yl = r % NX, r // NX
    z, yh = m // NYH, m % NYH
    row_dev = lambda a, b: (((yl + b) % NYL) * NX + (x + a) % NX, c)
    key_dev = lambda a, b: (r, (((z + a) % NZ) * NYH + (yh + b) % NYH) * 2 + e)
    sib_dev = (r, m * 2 + 1 - e)
    diagonal = r == m

    def remote(src, dst, ss, rs, device):
        return pltpu.make_async_remote_copy(
            src_ref=src, dst_ref=dst, send_sem=ss, recv_sem=rs, device_id=device, device_id_type=MESH
        )

    barrier = pltpu.get_barrier_semaphore()
    pl.semaphore_signal(barrier, inc=1, device_id=sib_dev, device_id_type=MESH)
    for a, b in shifts():
        pl.semaphore_signal(barrier, inc=1, device_id=row_dev(a, b), device_id_type=MESH)
        pl.semaphore_signal(barrier, inc=1, device_id=key_dev(a, b), device_id_type=MESH)
    for k in range(NM):
        @pl.when(jnp.logical_not(diagonal & (m == k)))
        def _():
            pl.semaphore_signal(barrier, inc=1, device_id=(m, k * 2 + e), device_id_type=MESH)

    local_bias = pltpu.make_async_copy(bias_ref.at[:, pl.ds(pl.multiple_of(e * CHUNK, CHUNK), CHUNK), :], braw.at[e], bias_ls)
    local_bias.start()

    values = x_ref[0].astype(F32)
    average = jnp.mean(values, axis=-1, keepdims=True)
    centred = values - average
    variance = jnp.mean(centred * centred, axis=-1, keepdims=True)
    normed = (centred * lax.rsqrt(variance + epsilon) * gain_ref[...]).astype(BF16)
    own[...] = normed
    nbuf[r, e] = normed

    pl.semaphore_wait(barrier, 15 + jnp.where(diagonal, NR - 1, NR))

    q_send = remote(own, qbuf.at[r], t_ss, q_rs.at[r], (m, r * 2 + e))

    @pl.when(jnp.logical_not(diagonal))
    def _():
        q_send.start()

    @pl.when(diagonal)
    def _():
        qbuf[r] = own[...]

    kv_sends = [
        remote(own, nbuf.at[r, e], kv_ss.at[n], kv_rs.at[r], row_dev(a, b)) for n, (a, b) in enumerate(shifts())
    ]
    for send in kv_sends:
        send.start()
    remote(own, nbuf.at[r, e], sib_ss.at[r], sib_rs.at[r], sib_dev).start()
    bias_send = remote(
        bias_ref.at[:, pl.ds(pl.multiple_of((1 - e) * CHUNK, CHUNK), CHUNK), :], braw.at[e], bias_ss, bias_rs, sib_dev
    )
    bias_send.start()

    def forward(i):
        @pl.when(i != r)
        def _():
            remote(own, nbuf.at[i, e], kv_ss.at[0], kv_rs.at[i], sib_dev).wait_recv()
            remote(nbuf.at[i, e], nbuf.at[i, e], sib_ss.at[i], sib_rs.at[i], sib_dev).start()

    def turn_bias(core):
        for b in range(2):
            key0 = m * 512 + core * CHUNK + b * KEYBLK
            place = key0 + lax.broadcasted_iota(jnp.int32, (1, KEYBLK), 1)
            inside = jnp.zeros((1, KEYBLK), jnp.bool_)
            leading = jnp.zeros((1, KEYBLK), jnp.bool_)
            for n in range(4):
                start = starts_ref[n]
                end = (starts_ref[n + 1] if n < 3 else 4096) - pads_ref[n]
                inside = inside | ((place >= start) & (place < end))
                leading = leading | (place == start)
            alive = inside & ((mask_ref[m, pl.ds(core * 2 + b, 1), :] == 1) | leading)
            for h in range(HEADS):
                piece = braw[core, h, :, b * KEYBLK : (b + 1) * KEYBLK].astype(F32)
                piece = jnp.where(alive, piece, dead_bias)
                biasT[h, pl.ds(pl.multiple_of(core * CHUNK + b * KEYBLK, KEYBLK), KEYBLK), :] = piece.T

    local_bias.wait()
    turn_bias(e)

    @pl.when(jnp.logical_not(diagonal))
    def _():
        remote(own, qbuf.at[m], t_ss, q_rs.at[m], sib_dev).wait_recv()

    q_sends = [
        remote(qbuf.at[m], qbuf.at[m], q_ss.at[n], q_rs.at[m], key_dev(a, b)) for n, (a, b) in enumerate(shifts())
    ]
    for send in q_sends:
        send.start()
    bias_send.wait_recv()
    turn_bias(1 - e)
    forward(m)

    def step(s, carry):
        i = (m + s) % NR

        @pl.when(s < NR - 1)
        def _():
            forward((i + 1) % NR)

        remote(own, nbuf.at[i, 1 - e], kv_ss.at[0], sib_rs.at[i], sib_dev).wait_recv()

        @pl.when(s > 0)
        def _():
            remote(own, qbuf.at[i], kv_ss.at[0], q_rs.at[i], sib_dev).wait_recv()

        rows = nbuf[i].reshape(2 * CHUNK, CH)
        keys = jnp.dot(rows, wk_ref[...], preferred_element_type=F32).astype(BF16)
        valuesT = contract(wvT_ref[...], rows, 1, 1).astype(BF16)
        queriesT = (contract(wqT_ref[...], qbuf[i], 1, 1) * (WIDTH**-0.5)).astype(BF16)
        for h in range(HEADS):
            low = h * WIDTH
            parts = []
            if low:
                parts.append(jnp.zeros((low, CHUNK), BF16))
            parts.append(queriesT[low : low + WIDTH])
            if low + WIDTH < CH:
                parts.append(jnp.zeros((CH - low - WIDTH, CHUNK), BF16))
            one_head = jnp.concatenate(parts, axis=0)
            maxima, sums, accs = [], [], []
            for b in range(4):
                k0 = b * KEYBLK
                scores = jnp.dot(keys[k0 : k0 + KEYBLK], one_head, preferred_element_type=F32)
                scores = scores + biasT[h, k0 : k0 + KEYBLK, :]
                block_max = jnp.maximum(jnp.max(scores, axis=0, keepdims=True), dead_score)
                weights = jnp.exp(scores - block_max)
                sums.append(jnp.sum(weights, axis=0, keepdims=True))
                accs.append(
                    jnp.dot(valuesT[low : low + WIDTH, k0 : k0 + KEYBLK], weights.astype(BF16), preferred_element_type=F32)
                )
                maxima.append(block_max)
            top = functools.reduce(jnp.maximum, maxima)
            factors = [jnp.exp(v - top) for v in maxima]
            total = sum(f * v for f, v in zip(factors, sums))
            accum = sum(f * v for f, v in zip(factors, accs))
            sbuf[i, low : low + WIDTH, :] = accum
            sbuf[i, STAT + h : STAT + h + 1, :] = top
            sbuf[i, STAT + HEADS + h : STAT + HEADS + h + 1, :] = total

        at_home = diagonal & (i == r)

        @pl.when(at_home)
        def _():
            pltpu.make_async_copy(sbuf.at[i], rbuf.at[m], home_ls).start()

        @pl.when(jnp.logical_not(at_home))
        def _():
            remote(sbuf.at[i], rbuf.at[m], home_ss.at[i], home_rs.at[m], (i, r * 2 + e)).start()

        return carry

    lax.fori_loop(0, NR, step, 0)

    gatesT = contract(wgT_ref[...], own[...], 1, 1).astype(BF16).astype(F32)

    for k in range(NM):
        is_self = diagonal & (m == k)

        @pl.when(is_self)
        def _():
            pltpu.make_async_copy(sbuf.at[k], rbuf.at[k], home_ls).wait()

        @pl.when(jnp.logical_not(is_self))
        def _():
            remote(sbuf.at[k], rbuf.at[k], home_ss.at[k], home_rs.at[k], sib_dev).wait_recv()

    gated = []
    for h in range(HEADS):
        low = h * WIDTH
        tops = [rbuf[k, STAT + h : STAT + h + 1, :] for k in range(NM)]
        top = functools.reduce(jnp.maximum, tops)
        factors = [jnp.exp(v - top) for v in tops]
        total = sum(f * rbuf[k, STAT + HEADS + h : STAT + HEADS + h + 1, :] for k, f in enumerate(factors))
        accum = sum(f * rbuf[k, low : low + WIDTH, :] for k, f in enumerate(factors))
        attended = accum / total
        gate = 1.0 / (1.0 + jnp.exp(-gatesT[low : low + WIDTH]))
        gated.append((gate * attended).astype(BF16))
    gatedT = jnp.concatenate(gated, axis=0)
    out_ref[0] = contract(gatedT, w_out_ref[...], 0, 0).astype(BF16)

    for send in kv_sends + q_sends:
        send.wait_send()
    bias_send.wait_send()

    @pl.when(jnp.logical_not(diagonal))
    def _():
        q_send.wait_send()

    for k in range(NR):
        remote(own, nbuf.at[k, e], sib_ss.at[k], sib_rs.at[k], sib_dev).wait_send()

        @pl.when(jnp.logical_not(diagonal & (m == k)))
        def _():
            remote(sbuf.at[k], rbuf.at[k], home_ss.at[k], home_rs.at[k], sib_dev).wait_send()


def local(pair_window, ln_gain, w_proj, w_out, pair_bias, chain_starts, chain_pads, residue_mask):
    vmem = pl.BlockSpec(memory_space=pltpu.VMEM)
    smem = pl.BlockSpec(memory_space=pltpu.SMEM)
    dma = pltpu.SemaphoreType.DMA
    wT = w_proj.T
    return pl.pallas_call(
        kernel,
        out_shape=jax.ShapeDtypeStruct((1, CHUNK, CH), BF16),
        in_specs=[smem, smem] + [vmem] * 8 + [pl.BlockSpec(memory_space=pl.ANY)],
        out_specs=vmem,
        scratch_shapes=[
            pltpu.VMEM((NR, 2, CHUNK, CH), BF16),
            pltpu.VMEM((NR, CHUNK, CH), BF16),
            pltpu.VMEM((2, HEADS, CHUNK, CHUNK), BF16),
            pltpu.VMEM((HEADS, 2 * CHUNK, CHUNK), F32),
            pltpu.VMEM((CHUNK, CH), BF16),
            pltpu.VMEM((NR, MSG, CHUNK), F32),
            pltpu.VMEM((NM, MSG, CHUNK), F32),
            dma((7,)), dma((NR,)), dma((NR,)), dma((NR,)), dma((7,)), dma((NR,)), dma, dma, dma, dma,
            dma((NR,)), dma((NM,)), dma,
        ],
        compiler_params=pltpu.CompilerParams(
            collective_id=0, has_side_effects=True, vmem_limit_bytes=40 * 2**20
        ),
        name="triangle",
    )(
        chain_starts, chain_pads, pair_window, ln_gain.reshape(1, CH), wT[:CH], w_proj[:, CH : 2 * CH],
        wT[2 * CH : 3 * CH], wT[3 * CH :], w_out, residue_mask.reshape(NM, 4, 128), pair_bias,
    )


def solution(mesh):
    in_specs = (P("row", "key", None), P(), P(), P(), P(None, "row", "key"), P(), P(), P())
    out_specs = P("row", "key", None)
    return jax.shard_map(local, mesh=mesh, in_specs=in_specs, out_specs=out_specs, check_vma=False)
```

time: 679 us -> 75.7 us (0.11)
  the two profiles are of different devices: /device:TPU:0 before, /device:TPU:32 now
where the time goes in v1:
time: 75.7 us; the launch traced here: 75.5 us
  Pallas kernels  71.1 us (94%)
  local copies, waits for them, and re-layouts  4.36 us (6%)
    pallas_call x1, Pallas kernels, local(): pl.pallas_call(kernel, out_shape=jax.ShapeDtypeStruct((1, CHUNK, CH), BF1...  71.1 us
    unnamed x16, local copies, waits for them, and re-layouts  3.56 us

profile of v1, /device:TPU:32, one launch (start us, length us, event | category | flops | bytes accessed | tf_op | source)
XLA Modules:
  0.0 75.5 jit_solution(16720677222272776799)
XLA Ops:
  0.0 1.0 %copy.9 = bf16[128,512]{0,1:T(8,128)(2,1)S(1)} copy(bf16[128,512]{1,0:T(8,128)(2,1)} %param.10) | data formatting | bytes 262144 | tf_op args[2]
  1.0 0.0 copy-start.2
  1.0 0.0 copy-start.3
  1.1 0.0 copy-start.1
  1.1 0.8 %slice.13.wk_ref = bf16[128,128]{1,0:T(8,128)(2,1)S(1)} slice(bf16[128,512]{1,0:T(8,128)(2,1)} %param.10), slice={[0:128], [128:256]} | slice | bytes 65536 | tf_op jit(solution)/shard_map/slice | solution.py:270
  1.9 0.0 copy-start.4
  1.9 0.0 copy-start.5
  1.9 0.0 copy-start.6
  1.9 0.0 copy-done.2
  1.9 0.0 copy-done.3
  1.9 0.0 copy-done.1
  1.9 0.6 copy-done.4
  2.5 0.0 copy-done.5
  2.6 0.0 copy-done.6
  2.6 0.0 copy-start
  2.6 1.2 %copy-done = bf16[4,512,256]{2,1,0:T(8,128)(2,1)S(1)} copy-done((bf16[4,512,256]{2,1,0:T(8,128)(2,1)S(1)}, bf16[4,512,256]{2,1,0:T(8,128)(2,1)}, u32[]{:S(2)}) %copy-start) | copy-done | bytes 1048600
  3.8 71.1 %triangle.1 = bf16[1,256,128]{2,1,0:T(8,128)(2,1)S(1)} custom-call(s32[4]{0:T(128)S(1)} %copy-done.4, s32[4]{0:T(128)S(1)} %copy-done.5, bf16[1,256,128]{2,1,0:T(8,128)(2,1)S(1)} %copy-done.1, f32[1,128]{1,0:T(1,128)S(1)} %bitcast.4, bf16[128,128]{1,0:T(8,128)(2,1)S(1)} %get-tuple-element.7.wqT_ref, bf16[128,128]{1,0:T(8,128)(2,1)S(1)} %slice.13.wk_ref, ...), custom_call_target="tpu_custom_call" | custom-call | tf_op jit(solution)/shard_map/triangle/pallas_call | solution.py:249
  74.9 0.6 copy.11
  (1 shorter events, 0.0 us)
Async XLA Ops:
  1.0 0.9 %copy-start.2 = (bf16[128,128]{1,0:T(8,128)(2,1)S(1)}, bf16[128,128]{1,0:T(8,128)(2,1)}, u32[]{:S(2)}) copy-start(bf16[128,128]{1,0:T(8,128)(2,1)} %w_out_ref.1) | copy-start | bytes 98308
  1.0 0.9 %copy-start.3 = (s32[4096]{0:T(1024)S(1)}, s32[4096]{0:T(1024)}, u32[]{:S(2)}) copy-start(s32[4096]{0:T(1024)} %param.15) | copy-start | bytes 49156
  1.1 0.8 %copy-start.1 = (bf16[1,256,128]{2,1,0:T(8,128)(2,1)S(1)}, bf16[1,256,128]{2,1,0:T(8,128)(2,1)}, u32[]{:S(2)}) copy-start(bf16[1,256,128]{2,1,0:T(8,128)(2,1)} %x_ref.1) | copy-start | bytes 196612
  1.9 0.7 copy-start.4
  1.9 0.7 copy-start.5
  1.9 0.7 copy-start.6
  2.6 1.2 %copy-start = (bf16[4,512,256]{2,1,0:T(8,128)(2,1)S(1)}, bf16[4,512,256]{2,1,0:T(8,128)(2,1)}, u32[]{:S(2)}) copy-start(bf16[4,512,256]{2,1,0:T(8,128)(2,1)} %bias_ref.1) | copy-start | bytes 3145732

commit v2 on v1

v2 whole, which is shorter than its diff:
```python
import functools

import jax
import jax.numpy as jnp
from jax import lax
from jax.experimental import pallas as pl
from jax.experimental.pallas import tpu as pltpu
from jax.sharding import PartitionSpec as P

HEADS = 4
KEYBLK = 128
WIDTH = 32
CH = 128
CHUNK = 256
KEYS = 2 * CHUNK
NBLK = KEYS // KEYBLK
NX, NYL, NZ, NYH = 4, 2, 4, 2
NR = NX * NYL
NM = NZ * NYH
NCHAIN = 4
LENGTH = 4096
STATS = 16
STEPS = 32767.0
MESH = pl.DeviceIdType.MESH
F32 = jnp.float32
BF16 = jnp.bfloat16

epsilon = 1e-05
dead_score = -1000000000.0
dead_bias = -1e30


def contract(a, b, dim_a, dim_b):
    return lax.dot_general(a, b, (((dim_a,), (dim_b,)), ((), ())), preferred_element_type=F32)


def kernel(
    starts_ref, pads_ref, x_hbm, gain_hbm, w_hbm, w_out_hbm, mask_hbm, bias_ref, out_ref,
    x_ref, gain_ref, w_ref, w_out_ref, mask_ref,
    nbuf, qbuf, braw, biasT, own, wqT, wvT, wgT, s_scr, p_scr, sbuf, sstat, rbuf, rstat,
    in_sem, kv_ss, kv_rs, sib_ss, sib_rs, q_ss, q_rs, t_ss, bias_ss, bias_rs, bias_ls, home_ss, home_rs, home_ls,
    stat_ss, stat_rs, stat_ls,
):
    r = lax.axis_index("row")
    c = lax.axis_index("key")
    m = c // 2
    e = c % 2
    x, yl = r % NX, r // NX
    z, yh = m // NYH, m % NYH
    row_at = lambda a, b: ((yl + b) % NYL) * NX + (x + a) % NX
    key_at = lambda a, b: ((z + a) % NZ) * NYH + (yh + b) % NYH
    row_dev = lambda a, b: (row_at(a, b), c)
    key_dev = lambda a, b: (r, key_at(a, b) * 2 + e)
    sib_dev = (r, m * 2 + 1 - e)
    diagonal = r == m

    def remote(src, dst, ss, rs, device):
        return pltpu.make_async_remote_copy(
            src_ref=src, dst_ref=dst, send_sem=ss, recv_sem=rs, device_id=device, device_id_type=MESH
        )

    loads = [
        pltpu.make_async_copy(src, dst, in_sem.at[n])
        for n, (src, dst) in enumerate(
            ((x_hbm, x_ref), (gain_hbm, gain_ref), (w_hbm, w_ref), (w_out_hbm, w_out_ref), (mask_hbm, mask_ref))
        )
    ]
    for load in loads:
        load.start()
    local_bias = pltpu.make_async_copy(bias_ref.at[:, pl.ds(pl.multiple_of(e * CHUNK, CHUNK), CHUNK), :], braw.at[e], bias_ls)
    local_bias.start()

    barrier = pltpu.get_barrier_semaphore()
    pl.semaphore_signal(barrier, inc=1, device_id=sib_dev, device_id_type=MESH)
    for a, b in ((1, 0), (2, 0), (3, 0), (0, 1)):
        pl.semaphore_signal(barrier, inc=1, device_id=row_dev(a, b), device_id_type=MESH)
        pl.semaphore_signal(barrier, inc=1, device_id=key_dev(a, b), device_id_type=MESH)
    for k in range(NM):
        @pl.when(jnp.logical_not(diagonal & (m == k)))
        def _():
            pl.semaphore_signal(barrier, inc=1, device_id=(m, k * 2 + e), device_id_type=MESH)

    loads[0].wait()
    loads[1].wait()
    values = x_ref[0].astype(F32)
    average = jnp.mean(values, axis=-1, keepdims=True)
    centred = values - average
    variance = jnp.mean(centred * centred, axis=-1, keepdims=True)
    normed = (centred * lax.rsqrt(variance + epsilon) * gain_ref[...]).astype(BF16)
    own[...] = normed
    nbuf[r, e] = normed

    pl.semaphore_wait(barrier, 9 + jnp.where(diagonal, NR - 1, NR))

    q_send = remote(own, qbuf.at[r], t_ss, q_rs.at[r], (m, r * 2 + e))

    @pl.when(jnp.logical_not(diagonal))
    def _():
        q_send.start()

    @pl.when(diagonal)
    def _():
        qbuf[r] = own[...]

    partner = row_at(0, 1)
    kv_sends = [remote(own, nbuf.at[r, e], kv_ss.at[0], kv_rs.at[r], row_dev(0, 1))]
    kv_sends += [remote(own, nbuf.at[r, e], kv_ss.at[a], kv_rs.at[r], row_dev(a, 0)) for a in (1, 3, 2)]
    for send in kv_sends:
        send.start()
    remote(own, nbuf.at[r, e], sib_ss.at[r], sib_rs.at[r], sib_dev).start()
    bias_send = remote(
        bias_ref.at[:, pl.ds(pl.multiple_of((1 - e) * CHUNK, CHUNK), CHUNK), :], braw.at[e], bias_ss, bias_rs, sib_dev
    )
    bias_send.start()

    def arrived(i):
        remote(own, nbuf.at[i, e], kv_ss.at[0], kv_rs.at[i], sib_dev).wait_recv()

    def to_sibling(i):
        @pl.when((i != r) & (i != partner))
        def _():
            arrived(i)
            remote(nbuf.at[i, e], nbuf.at[i, e], sib_ss.at[i], sib_rs.at[i], sib_dev).start()

    loads[2].wait()
    for ref, low in ((wqT, 0), (wvT, 2 * CH), (wgT, 3 * CH)):
        ref[...] = w_ref[:, low : low + CH].astype(F32).T.astype(BF16)
    loads[4].wait()

    def turn_bias(core):
        for b in range(2):
            key0 = m * KEYS + core * CHUNK + b * KEYBLK
            place = key0 + lax.broadcasted_iota(jnp.int32, (1, KEYBLK), 1)
            inside = jnp.zeros((1, KEYBLK), jnp.bool_)
            leading = jnp.zeros((1, KEYBLK), jnp.bool_)
            for n in range(NCHAIN):
                start = starts_ref[n]
                end = (starts_ref[n + 1] if n < NCHAIN - 1 else LENGTH) - pads_ref[n]
                inside = inside | ((place >= start) & (place < end))
                leading = leading | (place == start)
            alive = inside & ((mask_ref[pl.ds(m * NBLK + core * 2 + b, 1), :] == 1) | leading)
            for h in range(HEADS):
                piece = braw[core, h, :, b * KEYBLK : (b + 1) * KEYBLK].astype(F32)
                piece = jnp.where(alive, piece, dead_bias)
                biasT[h, pl.ds(pl.multiple_of(core * CHUNK + b * KEYBLK, KEYBLK), KEYBLK), :] = piece.T

    local_bias.wait()
    turn_bias(e)

    arrived(partner)
    kv_ons = [remote(nbuf.at[partner, e], nbuf.at[partner, e], kv_ss.at[3 + a], kv_rs.at[partner], row_dev(a, 0)) for a in (1, 3, 2)]
    for send in kv_ons:
        send.start()
    remote(nbuf.at[partner, e], nbuf.at[partner, e], sib_ss.at[partner], sib_rs.at[partner], sib_dev).start()

    def q_arrived(i):
        remote(own, qbuf.at[i], t_ss, q_rs.at[i], sib_dev).wait_recv()

    @pl.when(jnp.logical_not(diagonal))
    def _():
        q_arrived(m)

    q_sends = [remote(qbuf.at[m], qbuf.at[m], q_ss.at[0], q_rs.at[m], key_dev(0, 1))]
    q_sends += [remote(qbuf.at[m], qbuf.at[m], q_ss.at[a], q_rs.at[m], key_dev(a, 0)) for a in (1, 3, 2)]
    for send in q_sends:
        send.start()
    bias_send.wait_recv()
    turn_bias(1 - e)
    to_sibling(m)

    other = key_at(0, 1)
    q_arrived(other)
    q_ons = [remote(qbuf.at[other], qbuf.at[other], q_ss.at[3 + a], q_rs.at[other], key_dev(a, 0)) for a in (1, 3, 2)]
    for send in q_ons:
        send.start()

    def turn(s):
        return ((z + s) % NZ) * NYH + (yh + s // NZ) % NYH

    def step(s, carry):
        i = turn(s)

        @pl.when(s < NR - 1)
        def _():
            to_sibling(turn(s + 1))

        remote(own, nbuf.at[i, 1 - e], kv_ss.at[0], sib_rs.at[i], sib_dev).wait_recv()

        @pl.when((s > 0) & (s != NZ))
        def _():
            q_arrived(i)

        rows = nbuf[i].reshape(KEYS, CH)
        keys = jnp.dot(rows, w_ref[:, CH : 2 * CH], preferred_element_type=F32).astype(BF16)
        valuesT = contract(wvT[...], rows, 1, 1).astype(BF16)
        queriesT = (contract(wqT[...], qbuf[i], 1, 1) * (WIDTH**-0.5)).astype(BF16)
        tops, sums = {}, {}

        def phase_scores(h):
            low = h * WIDTH
            parts = []
            if low:
                parts.append(jnp.zeros((low, CHUNK), BF16))
            parts.append(queriesT[low : low + WIDTH])
            if low + WIDTH < CH:
                parts.append(jnp.zeros((CH - low - WIDTH, CHUNK), BF16))
            one_head = jnp.concatenate(parts, axis=0)
            scores = jnp.dot(keys, one_head, preferred_element_type=F32)
            tops[h] = []
            for b in range(NBLK):
                k0 = b * KEYBLK
                part = scores[k0 : k0 + KEYBLK] + biasT[h, k0 : k0 + KEYBLK, :]
                s_scr[h, k0 : k0 + KEYBLK, :] = part
                tops[h].append(jnp.maximum(jnp.max(part, axis=0, keepdims=True), dead_score))

        def phase_weights(h):
            sums[h] = []
            for b in range(NBLK):
                k0 = b * KEYBLK
                weights = jnp.exp(s_scr[h, k0 : k0 + KEYBLK, :] - tops[h][b])
                sums[h].append(jnp.sum(weights, axis=0, keepdims=True))
                p_scr[h, k0 : k0 + KEYBLK, :] = weights.astype(BF16)

        def phase_values(h):
            low = h * WIDTH
            accs = []
            for b in range(NBLK):
                k0 = b * KEYBLK
                accs.append(
                    jnp.dot(valuesT[low : low + WIDTH, k0 : k0 + KEYBLK], p_scr[h, k0 : k0 + KEYBLK, :], preferred_element_type=F32)
                )
            top = functools.reduce(jnp.maximum, tops[h])
            factors = [jnp.exp(v - top) for v in tops[h]]
            total = sum(f * v for f, v in zip(factors, sums[h]))
            accum = sum(f * v for f, v in zip(factors, accs))
            reach = jnp.maximum(jnp.max(jnp.abs(accum), axis=0, keepdims=True), 1e-30)
            sbuf[i, low : low + WIDTH, :] = jnp.round(accum * (STEPS / reach)).astype(jnp.int32).astype(jnp.int16)
            sstat[i, h : h + 1, :] = top
            sstat[i, HEADS + h : HEADS + h + 1, :] = total
            sstat[i, 2 * HEADS + h : 2 * HEADS + h + 1, :] = reach * (1.0 / STEPS)

        for t in range(HEADS + 2):
            if t < HEADS:
                phase_scores(t)
            if 0 <= t - 1 < HEADS:
                phase_weights(t - 1)
            if 0 <= t - 2 < HEADS:
                phase_values(t - 2)

        at_home = diagonal & (i == r)

        @pl.when(at_home)
        def _():
            pltpu.make_async_copy(sbuf.at[i], rbuf.at[m], home_ls).start()
            pltpu.make_async_copy(sstat.at[i], rstat.at[m], stat_ls).start()

        @pl.when(jnp.logical_not(at_home))
        def _():
            remote(sbuf.at[i], rbuf.at[m], home_ss.at[i], home_rs.at[m], (i, r * 2 + e)).start()
            remote(sstat.at[i], rstat.at[m], stat_ss.at[i], stat_rs.at[m], (i, r * 2 + e)).start()

        return carry

    sstat[:, 3 * HEADS :, :] = jnp.zeros((NR, STATS - 3 * HEADS, CHUNK), F32)
    lax.fori_loop(0, NR, step, 0)

    gatesT = contract(wgT[...], own[...], 1, 1).astype(BF16).astype(F32)
    gates = 1.0 / (1.0 + jnp.exp(-gatesT))
    loads[3].wait()

    for k in range(NM):
        is_self = diagonal & (m == k)

        @pl.when(is_self)
        def _():
            pltpu.make_async_copy(sbuf.at[k], rbuf.at[k], home_ls).wait()
            pltpu.make_async_copy(sstat.at[k], rstat.at[k], stat_ls).wait()

        @pl.when(jnp.logical_not(is_self))
        def _():
            remote(sbuf.at[k], rbuf.at[k], home_ss.at[k], home_rs.at[k], sib_dev).wait_recv()
            remote(sstat.at[k], rstat.at[k], stat_ss.at[k], stat_rs.at[k], sib_dev).wait_recv()

    gated = []
    for h in range(HEADS):
        low = h * WIDTH
        tops = [rstat[k, h : h + 1, :] for k in range(NM)]
        top = functools.reduce(jnp.maximum, tops)
        factors = [jnp.exp(v - top) for v in tops]
        total = sum(f * rstat[k, HEADS + h : HEADS + h + 1, :] for k, f in enumerate(factors))
        accum = sum(
            (f * rstat[k, 2 * HEADS + h : 2 * HEADS + h + 1, :]) * rbuf[k, low : low + WIDTH, :].astype(jnp.int32).astype(F32)
            for k, f in enumerate(factors)
        )
        gated.append((gates[low : low + WIDTH] * (accum / total)).astype(BF16))
    gatedT = jnp.concatenate(gated, axis=0)
    out_ref[0] = contract(gatedT, w_out_ref[...], 0, 0).astype(BF16)

    for send in kv_sends + kv_ons + q_sends + q_ons:
        send.wait_send()
    bias_send.wait_send()

    @pl.when(jnp.logical_not(diagonal))
    def _():
        q_send.wait_send()

    for k in range(NR):
        remote(own, nbuf.at[k, e], sib_ss.at[k], sib_rs.at[k], sib_dev).wait_send()

        @pl.when(jnp.logical_not(diagonal & (m == k)))
        def _():
            remote(sbuf.at[k], rbuf.at[k], home_ss.at[k], home_rs.at[k], sib_dev).wait_send()
            remote(sstat.at[k], rstat.at[k], stat_ss.at[k], stat_rs.at[k], sib_dev).wait_send()


def local(pair_window, ln_gain, w_proj, w_out, pair_bias, chain_starts, chain_pads, residue_mask):
    vmem = pl.BlockSpec(memory_space=pltpu.VMEM)
    smem = pl.BlockSpec(memory_space=pltpu.SMEM)
    hbm = pl.BlockSpec(memory_space=pl.ANY)
    dma = pltpu.SemaphoreType.DMA
    return pl.pallas_call(
        kernel,
        out_shape=jax.ShapeDtypeStruct((1, CHUNK, CH), BF16),
        in_specs=[smem, smem] + [hbm] * 6,
        out_specs=vmem,
        scratch_shapes=[
            pltpu.VMEM((1, CHUNK, CH), BF16),
            pltpu.VMEM((1, CH), F32),
            pltpu.VMEM((CH, 4 * CH), BF16),
            pltpu.VMEM((CH, CH), BF16),
            pltpu.VMEM((LENGTH // KEYBLK, KEYBLK), jnp.int32),
            pltpu.VMEM((NR, 2, CHUNK, CH), BF16),
            pltpu.VMEM((NR, CHUNK, CH), BF16),
            pltpu.VMEM((2, HEADS, CHUNK, CHUNK), BF16),
            pltpu.VMEM((HEADS, KEYS, CHUNK), F32),
            pltpu.VMEM((CHUNK, CH), BF16),
            pltpu.VMEM((CH, CH), BF16),
            pltpu.VMEM((CH, CH), BF16),
            pltpu.VMEM((CH, CH), BF16),
            pltpu.VMEM((HEADS, KEYS, CHUNK), F32),
            pltpu.VMEM((HEADS, KEYS, CHUNK), BF16),
            pltpu.VMEM((NR, CH, CHUNK), jnp.int16),
            pltpu.VMEM((NR, STATS, CHUNK), F32),
            pltpu.VMEM((NM, CH, CHUNK), jnp.int16),
            pltpu.VMEM((NM, STATS, CHUNK), F32),
            dma((5,)), dma((7,)), dma((NR,)), dma((NR,)), dma((NR,)), dma((7,)), dma((NR,)), dma, dma, dma, dma,
            dma((NR,)), dma((NM,)), dma, dma((NR,)), dma((NM,)), dma,
        ],
        compiler_params=pltpu.CompilerParams(
            collective_id=0, has_side_effects=True, vmem_limit_bytes=60 * 2**20
        ),
        name="triangle",
    )(
        chain_starts, chain_pads, pair_window, ln_gain.reshape(1, CH), w_proj, w_out,
        residue_mask.reshape(LENGTH // KEYBLK, KEYBLK), pair_bias,
    )


def solution(mesh):
    in_specs = (P("row", "key", None), P(), P(), P(), P(None, "row", "key"), P(), P(), P())
    out_specs = P("row", "key", None)
    return jax.shard_map(local, mesh=mesh, in_specs=in_specs, out_specs=out_specs, check_vma=False)
```

time: 75.7 us -> 42.9 us (0.57)
  the two profiles are of different devices: /device:TPU:32 before, /device:TPU:1 now
where the time goes in v2:
time: 42.9 us; the launch traced here: 42.7 us
  Pallas kernels  41.2 us (96%)
  local copies, waits for them, and re-layouts  1.47 us (3%)
    pallas_call x1, Pallas kernels, local(): pl.pallas_call(kernel, out_shape=jax.ShapeDtypeStruct((1, CHUNK, CH), BF1...  41.2 us
    unnamed x1, local copies, waits for them, and re-layouts  1.47 us

profile of v2, /device:TPU:1, one launch (start us, length us, event | category | flops | bytes accessed | tf_op | source)
XLA Modules:
  0.0 42.7 jit_solution(6962741433929232222)
XLA Ops:
  0.0 41.2 %triangle.1 = bf16[1,256,128]{2,1,0:T(8,128)(2,1)} custom-call(s32[4]{0:T(128)} %starts_ref.1, s32[4]{0:T(128)} %pads_ref.1, bf16[1,256,128]{2,1,0:T(8,128)(2,1)} %x_hbm.1, f32[1,128]{1,0:T(1,128)} %bitcast.3, bf16[128,512]{1,0:T(8,128)(2,1)} %w_hbm.1, bf16[128,128]{1,0:T(8,128)(2,1)} %w_out_hbm.1, s32[32,128]{1,0:T(8,128)} %bitcast.2, ...), custom_call_target="tpu_custom_call" | custom-call | tf_op jit(solution)/shard_map/triangle/pallas_call | solution.py:321
  41.2 1.5 %copy.10 = bf16[1,256,128]{2,1,0:T(8,128)(2,1)} copy(bf16[1,256,128]{2,1,0:T(8,128)(2,1)} %triangle.1) | data formatting | bytes 131072

commit v3 on v2

--- a/solution.py
+++ b/solution.py
@@ -37,7 +37,7 @@
 def kernel(
     starts_ref, pads_ref, x_hbm, gain_hbm, w_hbm, w_out_hbm, mask_hbm, bias_ref, out_ref,
     x_ref, gain_ref, w_ref, w_out_ref, mask_ref,
-    nbuf, qbuf, braw, biasT, own, wqT, wvT, wgT, s_scr, p_scr, sbuf, sstat, rbuf, rstat,
+    nbuf, qbuf, braw, biasT, own, wqT, wvT, wgT, s_scr, p_scr, sbuf, sstat, rbuf, rstat, merged,
     in_sem, kv_ss, kv_rs, sib_ss, sib_rs, q_ss, q_rs, t_ss, bias_ss, bias_rs, bias_ls, home_ss, home_rs, home_ls,
     stat_ss, stat_rs, stat_ls,
 ):
@@ -65,10 +65,9 @@
             ((x_hbm, x_ref), (gain_hbm, gain_ref), (w_hbm, w_ref), (w_out_hbm, w_out_ref), (mask_hbm, mask_ref))
         )
     ]
-    for load in loads:
-        load.start()
+    loads[0].start()
+    loads[1].start()
     local_bias = pltpu.make_async_copy(bias_ref.at[:, pl.ds(pl.multiple_of(e * CHUNK, CHUNK), CHUNK), :], braw.at[e], bias_ls)
-    local_bias.start()
 
     barrier = pltpu.get_barrier_semaphore()
     pl.semaphore_signal(barrier, inc=1, device_id=sib_dev, device_id_type=MESH)
@@ -79,6 +78,9 @@
         @pl.when(jnp.logical_not(diagonal & (m == k)))
         def _():
             pl.semaphore_signal(barrier, inc=1, device_id=(m, k * 2 + e), device_id_type=MESH)
+
+    for load in loads[2:] + [local_bias]:
+        load.start()
 
     loads[0].wait()
     loads[1].wait()
@@ -92,11 +94,14 @@
 
     pl.semaphore_wait(barrier, 9 + jnp.where(diagonal, NR - 1, NR))
 
-    q_send = remote(own, qbuf.at[r], t_ss, q_rs.at[r], (m, r * 2 + e))
+    HALF = CHUNK // 2
+    halves = [pl.ds(n * HALF, HALF) for n in range(2)]
+    t_sends = [remote(own.at[v], qbuf.at[r, v], t_ss.at[n], q_rs.at[n, r], (m, r * 2 + e)) for n, v in enumerate(halves)]
 
     @pl.when(jnp.logical_not(diagonal))
     def _():
-        q_send.start()
+        for send in t_sends:
+            send.start()
 
     @pl.when(diagonal)
     def _():
@@ -117,10 +122,8 @@
         remote(own, nbuf.at[i, e], kv_ss.at[0], kv_rs.at[i], sib_dev).wait_recv()
 
     def to_sibling(i):
-        @pl.when((i != r) & (i != partner))
-        def _():
-            arrived(i)
-            remote(nbuf.at[i, e], nbuf.at[i, e], sib_ss.at[i], sib_rs.at[i], sib_dev).start()
+        arrived(i)
+        remote(nbuf.at[i, e], nbuf.at[i, e], sib_ss.at[i], sib_rs.at[i], sib_dev).start()
 
     loads[2].wait()
     for ref, low in ((wqT, 0), (wvT, 2 * CH), (wgT, 3 * CH)):
@@ -153,26 +156,36 @@
         send.start()
     remote(nbuf.at[partner, e], nbuf.at[partner, e], sib_ss.at[partner], sib_rs.at[partner], sib_dev).start()
 
-    def q_arrived(i):
-        remote(own, qbuf.at[i], t_ss, q_rs.at[i], sib_dev).wait_recv()
-
-    @pl.when(jnp.logical_not(diagonal))
-    def _():
-        q_arrived(m)
-
-    q_sends = [remote(qbuf.at[m], qbuf.at[m], q_ss.at[0], q_rs.at[m], key_dev(0, 1))]
-    q_sends += [remote(qbuf.at[m], qbuf.at[m], q_ss.at[a], q_rs.at[m], key_dev(a, 0)) for a in (1, 3, 2)]
-    for send in q_sends:
-        send.start()
+    def q_arrived(i, n):
+        remote(own.at[halves[n]], qbuf.at[i, halves[n]], t_ss.at[0], q_rs.at[n, i], sib_dev).wait_recv()
+
+    def q_copy(i, n, slot, device):
+        v = qbuf.at[i, halves[n]]
+        return remote(v, v, q_ss.at[n, slot], q_rs.at[n, i], device)
+
+    q_sends = []
+    for n in range(2):
+        @pl.when(jnp.logical_not(diagonal))
+        def _():
+            q_arrived(m, n)
+
+        now = [q_copy(m, n, 0, key_dev(0, 1))] + [q_copy(m, n, a, key_dev(a, 0)) for a in (1, 3, 2)]
+        for send in now:
+            send.start()
+        q_sends += now
     bias_send.wait_recv()
     turn_bias(1 - e)
-    to_sibling(m)
+    for a, b in ((1, 0), (3, 0), (2, 0), (1, 1), (3, 1), (2, 1)):
+        to_sibling(row_at(a, b))
 
     other = key_at(0, 1)
-    q_arrived(other)
-    q_ons = [remote(qbuf.at[other], qbuf.at[other], q_ss.at[3 + a], q_rs.at[other], key_dev(a, 0)) for a in (1, 3, 2)]
-    for send in q_ons:
-        send.start()
+    q_ons = []
+    for n in range(2):
+        q_arrived(other, n)
+        now = [q_copy(other, n, 3 + a, key_dev(a, 0)) for a in (1, 3, 2)]
+        for send in now:
+            send.start()
+        q_ons += now
 
     def turn(s):
         return ((z + s) % NZ) * NYH + (yh + s // NZ) % NYH
@@ -180,15 +193,12 @@
     def step(s, carry):
         i = turn(s)
 
-        @pl.when(s < NR - 1)
-        def _():
-            to_sibling(turn(s + 1))
-
         remote(own, nbuf.at[i, 1 - e], kv_ss.at[0], sib_rs.at[i], sib_dev).wait_recv()
 
         @pl.when((s > 0) & (s != NZ))
         def _():
-            q_arrived(i)
+            q_arrived(i, 0)
+            q_arrived(i, 1)
 
         rows = nbuf[i].reshape(KEYS, CH)
         keys = jnp.dot(rows, w_ref[:, CH : 2 * CH], preferred_element_type=F32).astype(BF16)
@@ -268,7 +278,7 @@
     gates = 1.0 / (1.0 + jnp.exp(-gatesT))
     loads[3].wait()
 
-    for k in range(NM):
+    def home_arrived(k):
         is_self = diagonal & (m == k)
 
         @pl.when(is_self)
@@ -281,18 +291,39 @@
             remote(sbuf.at[k], rbuf.at[k], home_ss.at[k], home_rs.at[k], sib_dev).wait_recv()
             remote(sstat.at[k], rstat.at[k], stat_ss.at[k], stat_rs.at[k], sib_dev).wait_recv()
 
-    gated = []
+    def merge(group, so_far):
+        out = []
+        for h in range(HEADS):
+            low = h * WIDTH
+            tops = [rstat[k, h : h + 1, :] for k in group]
+            sums = [rstat[k, HEADS + h : HEADS + h + 1, :] for k in group]
+            if so_far is not None:
+                tops.append(so_far[h][0])
+                sums.append(so_far[h][1])
+            top = functools.reduce(jnp.maximum, tops)
+            factors = [jnp.exp(v - top) for v in tops]
+            total = sum(f * v for f, v in zip(factors, sums))
+            accum = sum(
+                (f * rstat[k, 2 * HEADS + h : 2 * HEADS + h + 1, :]) * rbuf[k, low : low + WIDTH, :].astype(jnp.int32).astype(F32)
+                for k, f in zip(group, factors)
+            )
+            if so_far is not None:
+                accum = accum + factors[-1] * merged[low : low + WIDTH, :]
+            out.append((top, total, accum))
+        return out
+
+    senders = [((r // NYH - a + NZ) % NZ) * NYH + (r + b) % NYH for b in range(NYH) for a in range(NZ)]
+    for k in senders[:6]:
+        home_arrived(k)
+    early = merge(senders[:6], None)
     for h in range(HEADS):
-        low = h * WIDTH
-        tops = [rstat[k, h : h + 1, :] for k in range(NM)]
-        top = functools.reduce(jnp.maximum, tops)
-        factors = [jnp.exp(v - top) for v in tops]
-        total = sum(f * rstat[k, HEADS + h : HEADS + h + 1, :] for k, f in enumerate(factors))
-        accum = sum(
-            (f * rstat[k, 2 * HEADS + h : 2 * HEADS + h + 1, :]) * rbuf[k, low : low + WIDTH, :].astype(jnp.int32).astype(F32)
-            for k, f in enumerate(factors)
-        )
-        gated.append((gates[low : low + WIDTH] * (accum / total)).astype(BF16))
+        merged[h * WIDTH : (h + 1) * WIDTH, :] = early[h][2]
+    for k in senders[6:]:
+        home_arrived(k)
+    gated = [
+        (gates[h * WIDTH : (h + 1) * WIDTH] * (accum / total)).astype(BF16)
+        for h, (top, total, accum) in enumerate(merge(senders[6:], early))
+    ]
     gatedT = jnp.concatenate(gated, axis=0)
     out_ref[0] = contract(gatedT, w_out_ref[...], 0, 0).astype(BF16)
 
@@ -302,7 +333,8 @@
 
     @pl.when(jnp.logical_not(diagonal))
     def _():
-        q_send.wait_send()
+        for send in t_sends:
+            send.wait_send()
 
     for k in range(NR):
         remote(own, nbuf.at[k, e], sib_ss.at[k], sib_rs.at[k], sib_dev).wait_send()
@@ -343,7 +375,8 @@
             pltpu.VMEM((NR, STATS, CHUNK), F32),
             pltpu.VMEM((NM, CH, CHUNK), jnp.int16),
             pltpu.VMEM((NM, STATS, CHUNK), F32),
-            dma((5,)), dma((7,)), dma((NR,)), dma((NR,)), dma((NR,)), dma((7,)), dma((NR,)), dma, dma, dma, dma,
+            pltpu.VMEM((CH, CHUNK), F32),
+            dma((5,)), dma((7,)), dma((NR,)), dma((NR,)), dma((NR,)), dma((2, 7)), dma((2, NR)), dma((2,)), dma, dma, dma,
             dma((NR,)), dma((NM,)), dma, dma((NR,)), dma((NM,)), dma,
         ],
         compiler_params=pltpu.CompilerParams(

time: 42.9 us -> 40.8 us (0.951)
  the two profiles are of different devices: /device:TPU:1 before, /device:TPU:0 now
where the time goes in v3:
time: 40.8 us; the launch traced here: 40.3 us
  Pallas kernels  38.8 us (95%)
  local copies, waits for them, and re-layouts  1.47 us (4%)
    pallas_call x1, Pallas kernels, local(): pl.pallas_call(kernel, out_shape=jax.ShapeDtypeStruct((1, CHUNK, CH), BF1...  38.8 us
    unnamed x1, local copies, waits for them, and re-layouts  1.47 us

profile of v3, /device:TPU:0, one launch (start us, length us, event | category | flops | bytes accessed | tf_op | source)
XLA Modules:
  0.0 40.3 jit_solution(3441530984887985407)
XLA Ops:
  0.0 38.8 %triangle.1 = bf16[1,256,128]{2,1,0:T(8,128)(2,1)} custom-call(s32[4]{0:T(128)} %starts_ref.1, s32[4]{0:T(128)} %pads_ref.1, bf16[1,256,128]{2,1,0:T(8,128)(2,1)} %x_hbm.1, f32[1,128]{1,0:T(1,128)} %bitcast.3, bf16[128,512]{1,0:T(8,128)(2,1)} %w_hbm.1, bf16[128,128]{1,0:T(8,128)(2,1)} %w_out_hbm.1, s32[32,128]{1,0:T(8,128)} %bitcast.2, ...), custom_call_target="tpu_custom_call" | custom-call | tf_op jit(solution)/shard_map/triangle/pallas_call | solution.py:353
  38.8 1.5 %copy.10 = bf16[1,256,128]{2,1,0:T(8,128)(2,1)} copy(bf16[1,256,128]{2,1,0:T(8,128)(2,1)} %triangle.1) | data formatting | bytes 131072

commit v4 on v3

--- a/solution.py
+++ b/solution.py
@@ -19,7 +19,7 @@
 NM = NZ * NYH
 NCHAIN = 4
 LENGTH = 4096
-STATS = 16
+STATS = 2 * HEADS
 STEPS = 32767.0
 MESH = pl.DeviceIdType.MESH
 F32 = jnp.float32
@@ -245,9 +245,9 @@
             accum = sum(f * v for f, v in zip(factors, accs))
             reach = jnp.maximum(jnp.max(jnp.abs(accum), axis=0, keepdims=True), 1e-30)
             sbuf[i, low : low + WIDTH, :] = jnp.round(accum * (STEPS / reach)).astype(jnp.int32).astype(jnp.int16)
-            sstat[i, h : h + 1, :] = top
-            sstat[i, HEADS + h : HEADS + h + 1, :] = total
-            sstat[i, 2 * HEADS + h : 2 * HEADS + h + 1, :] = reach * (1.0 / STEPS)
+            total = jnp.maximum(total, 1e-30)
+            sstat[i, h : h + 1, :] = top + jnp.log(total)
+            sstat[i, HEADS + h : HEADS + h + 1, :] = reach / (STEPS * total)
 
         for t in range(HEADS + 2):
             if t < HEADS:
@@ -271,7 +271,6 @@
 
         return carry
 
-    sstat[:, 3 * HEADS :, :] = jnp.zeros((NR, STATS - 3 * HEADS, CHUNK), F32)
     lax.fori_loop(0, NR, step, 0)
 
     gatesT = contract(wgT[...], own[...], 1, 1).astype(BF16).astype(F32)
@@ -296,15 +295,15 @@
         for h in range(HEADS):
             low = h * WIDTH
             tops = [rstat[k, h : h + 1, :] for k in group]
-            sums = [rstat[k, HEADS + h : HEADS + h + 1, :] for k in group]
             if so_far is not None:
                 tops.append(so_far[h][0])
-                sums.append(so_far[h][1])
             top = functools.reduce(jnp.maximum, tops)
             factors = [jnp.exp(v - top) for v in tops]
-            total = sum(f * v for f, v in zip(factors, sums))
+            total = sum(factors[: len(group)])
+            if so_far is not None:
+                total = total + factors[-1] * so_far[h][1]
             accum = sum(
-                (f * rstat[k, 2 * HEADS + h : 2 * HEADS + h + 1, :]) * rbuf[k, low : low + WIDTH, :].astype(jnp.int32).astype(F32)
+                (f * rstat[k, HEADS + h : HEADS + h + 1, :]) * rbuf[k, low : low + WIDTH, :].astype(jnp.int32).astype(F32)
                 for k, f in zip(group, factors)
             )
             if so_far is not None:
@@ -352,7 +351,7 @@
     dma = pltpu.SemaphoreType.DMA
     return pl.pallas_call(
         kernel,
-        out_shape=jax.ShapeDtypeStruct((1, CHUNK, CH), BF16),
+        out_shape=pltpu.VMEM((1, CHUNK, CH), BF16),
         in_specs=[smem, smem] + [hbm] * 6,
         out_specs=vmem,
         scratch_shapes=[

time: 40.8 us -> 38.7 us (0.949)
  Pallas kernels: 38.8 us -> 37.3 us
  local copies, waits for them, and re-layouts: 1.47 us -> 0.63 us
    pallas_call x1, Pallas kernels: 38.8 us -> 37.3 us  [local(): pl.pallas_call(kernel, out_shape=pltpu.VMEM((1, CHUNK, CH), BF16), in_spe...]
    unnamed x1, local copies, waits for them, and re-layouts: 1.47 us -> 0.63 us
where the time goes in v4:
time: 38.7 us; the launch traced here: 38 us
  Pallas kernels  37.3 us (96%)
  local copies, waits for them, and re-layouts  0.63 us (2%)
    pallas_call x1, Pallas kernels, local(): pl.pallas_call(kernel, out_shape=pltpu.VMEM((1, CHUNK, CH), BF16), in_spe...  37.3 us

profile of v4, /device:TPU:0, one launch (start us, length us, event | category | flops | bytes accessed | tf_op | source)
XLA Modules:
  0.0 38.0 jit_solution(14273779355388879280)
XLA Ops:
  0.0 37.3 %triangle.1 = bf16[1,256,128]{2,1,0:T(8,128)(2,1)S(1)} custom-call(s32[4]{0:T(128)} %starts_ref.1, s32[4]{0:T(128)} %pads_ref.1, bf16[1,256,128]{2,1,0:T(8,128)(2,1)} %x_hbm.1, f32[1,128]{1,0:T(1,128)} %bitcast.3, bf16[128,512]{1,0:T(8,128)(2,1)} %w_hbm.1, bf16[128,128]{1,0:T(8,128)(2,1)} %w_out_hbm.1, s32[32,128]{1,0:T(8,128)} %bitcast.2, ...), custom_call_target="tpu_custom_call" | custom-call | tf_op jit(solution)/shard_map/triangle/pallas_call | solution.py:352
  37.3 0.6 %copy.10 = bf16[1,256,128]{2,1,0:T(8,128)(2,1)} copy(bf16[1,256,128]{2,1,0:T(8,128)(2,1)S(1)} %triangle.1) | data formatting | bytes 131072

commit v5 on v4

--- a/solution.py
+++ b/solution.py
@@ -20,6 +20,7 @@
 NCHAIN = 4
 LENGTH = 4096
 STATS = 2 * HEADS
+HALF = CHUNK // 2
 STEPS = 32767.0
 MESH = pl.DeviceIdType.MESH
 F32 = jnp.float32
@@ -37,7 +38,7 @@
 def kernel(
     starts_ref, pads_ref, x_hbm, gain_hbm, w_hbm, w_out_hbm, mask_hbm, bias_ref, out_ref,
     x_ref, gain_ref, w_ref, w_out_ref, mask_ref,
-    nbuf, qbuf, braw, biasT, own, wqT, wvT, wgT, s_scr, p_scr, sbuf, sstat, rbuf, rstat, merged,
+    nbuf, qbuf, kbuf, vbuf, braw, biasT, own, wqT, wvT, wgT, s_scr, p_scr, sbuf, sstat, rbuf, rstat, merged,
     in_sem, kv_ss, kv_rs, sib_ss, sib_rs, q_ss, q_rs, t_ss, bias_ss, bias_rs, bias_ls, home_ss, home_rs, home_ls,
     stat_ss, stat_rs, stat_ls,
 ):
@@ -94,7 +95,6 @@
 
     pl.semaphore_wait(barrier, 9 + jnp.where(diagonal, NR - 1, NR))
 
-    HALF = CHUNK // 2
     halves = [pl.ds(n * HALF, HALF) for n in range(2)]
     t_sends = [remote(own.at[v], qbuf.at[r, v], t_ss.at[n], q_rs.at[n, r], (m, r * 2 + e)) for n, v in enumerate(halves)]
 
@@ -145,7 +145,11 @@
             for h in range(HEADS):
                 piece = braw[core, h, :, b * KEYBLK : (b + 1) * KEYBLK].astype(F32)
                 piece = jnp.where(alive, piece, dead_bias)
-                biasT[h, pl.ds(pl.multiple_of(core * CHUNK + b * KEYBLK, KEYBLK), KEYBLK), :] = piece.T
+                turned = piece.T
+                for n in range(2):
+                    biasT[
+                        n, h // 2, pl.ds(pl.multiple_of(core * CHUNK + b * KEYBLK, KEYBLK), KEYBLK), (h % 2) * HALF : (h % 2 + 1) * HALF
+                    ] = turned[:, n * HALF : (n + 1) * HALF]
 
     local_bias.wait()
     turn_bias(e)
@@ -190,64 +194,82 @@
     def turn(s):
         return ((z + s) % NZ) * NYH + (yh + s // NZ) % NYH
 
-    def step(s, carry):
-        i = turn(s)
-
-        remote(own, nbuf.at[i, 1 - e], kv_ss.at[0], sib_rs.at[i], sib_dev).wait_recv()
-
-        @pl.when((s > 0) & (s != NZ))
-        def _():
-            q_arrived(i, 0)
-            q_arrived(i, 1)
-
-        rows = nbuf[i].reshape(KEYS, CH)
-        keys = jnp.dot(rows, w_ref[:, CH : 2 * CH], preferred_element_type=F32).astype(BF16)
-        valuesT = contract(wvT[...], rows, 1, 1).astype(BF16)
-        queriesT = (contract(wqT[...], qbuf[i], 1, 1) * (WIDTH**-0.5)).astype(BF16)
+    def step(half, count, carry):
+        q_half = halves[half]
+        places = [2 * count + u for u in range(2)]
+        rows_i = [turn(s) for s in places]
+
+        for s, i in zip(places, rows_i):
+            if half == 0:
+                remote(own, nbuf.at[i, 1 - e], kv_ss.at[0], sib_rs.at[i], sib_dev).wait_recv()
+
+            @pl.when((s > 0) & (s != NZ))
+            def _():
+                remote(own.at[q_half], qbuf.at[i, q_half], t_ss.at[0], q_rs.at[half, i], sib_dev).wait_recv()
+
+        if half == 0:
+            for i in rows_i:
+                rows = nbuf[i].reshape(KEYS, CH)
+                kbuf[i] = jnp.dot(rows, w_ref[:, CH : 2 * CH], preferred_element_type=F32).astype(BF16)
+                vbuf[i] = contract(wvT[...], rows, 1, 1).astype(BF16)
+
+        queriesT = [(contract(wqT[...], qbuf[i, q_half, :], 1, 1) * (WIDTH**-0.5)).astype(BF16) for i in rows_i]
         tops, sums = {}, {}
 
-        def phase_scores(h):
+        def one_head(u, h):
             low = h * WIDTH
             parts = []
             if low:
-                parts.append(jnp.zeros((low, CHUNK), BF16))
-            parts.append(queriesT[low : low + WIDTH])
+                parts.append(jnp.zeros((low, HALF), BF16))
+            parts.append(queriesT[u][low : low + WIDTH])
             if low + WIDTH < CH:
-                parts.append(jnp.zeros((CH - low - WIDTH, CHUNK), BF16))
-            one_head = jnp.concatenate(parts, axis=0)
-            scores = jnp.dot(keys, one_head, preferred_element_type=F32)
-            tops[h] = []
+                parts.append(jnp.zeros((CH - low - WIDTH, HALF), BF16))
+            return jnp.concatenate(parts, axis=0)
+
+        def phase_scores(unit):
+            u, pair = unit // 2, unit % 2
+            both = jnp.concatenate([one_head(u, 2 * pair), one_head(u, 2 * pair + 1)], axis=1)
+            scores = jnp.dot(kbuf[rows_i[u]], both, preferred_element_type=F32)
+            tops[unit] = []
             for b in range(NBLK):
                 k0 = b * KEYBLK
-                part = scores[k0 : k0 + KEYBLK] + biasT[h, k0 : k0 + KEYBLK, :]
-                s_scr[h, k0 : k0 + KEYBLK, :] = part
-                tops[h].append(jnp.maximum(jnp.max(part, axis=0, keepdims=True), dead_score))
-
-        def phase_weights(h):
-            sums[h] = []
+                part = scores[k0 : k0 + KEYBLK] + biasT[half, pair, k0 : k0 + KEYBLK, :]
+                s_scr[unit, k0 : k0 + KEYBLK, :] = part
+                tops[unit].append(jnp.maximum(jnp.max(part, axis=0, keepdims=True), dead_score))
+
+        def phase_weights(unit):
+            sums[unit] = []
             for b in range(NBLK):
                 k0 = b * KEYBLK
-                weights = jnp.exp(s_scr[h, k0 : k0 + KEYBLK, :] - tops[h][b])
-                sums[h].append(jnp.sum(weights, axis=0, keepdims=True))
-                p_scr[h, k0 : k0 + KEYBLK, :] = weights.astype(BF16)
-
-        def phase_values(h):
-            low = h * WIDTH
+                weights = jnp.exp(s_scr[unit, k0 : k0 + KEYBLK, :] - tops[unit][b])
+                sums[unit].append(jnp.sum(weights, axis=0, keepdims=True))
+                p_scr[unit, k0 : k0 + KEYBLK, :] = weights.astype(BF16)
+
+        def phase_values(unit):
+            u, pair = unit // 2, unit % 2
+            i = rows_i[u]
+            low = 2 * pair * WIDTH
             accs = []
             for b in range(NBLK):
                 k0 = b * KEYBLK
-                accs.append(
-                    jnp.dot(valuesT[low : low + WIDTH, k0 : k0 + KEYBLK], p_scr[h, k0 : k0 + KEYBLK, :], preferred_element_type=F32)
+                both = jnp.dot(
+                    vbuf[i, low : low + 2 * WIDTH, k0 : k0 + KEYBLK], p_scr[unit, k0 : k0 + KEYBLK, :], preferred_element_type=F32
                 )
-            top = functools.reduce(jnp.maximum, tops[h])
-            factors = [jnp.exp(v - top) for v in tops[h]]
-            total = sum(f * v for f, v in zip(factors, sums[h]))
+                accs.append(jnp.concatenate([both[:WIDTH, :HALF], both[WIDTH:, HALF:]], axis=1))
+            top = functools.reduce(jnp.maximum, tops[unit])
+            factors = [jnp.exp(v - top) for v in tops[unit]]
+            total = jnp.maximum(sum(f * v for f, v in zip(factors, sums[unit])), 1e-30)
             accum = sum(f * v for f, v in zip(factors, accs))
             reach = jnp.maximum(jnp.max(jnp.abs(accum), axis=0, keepdims=True), 1e-30)
-            sbuf[i, low : low + WIDTH, :] = jnp.round(accum * (STEPS / reach)).astype(jnp.int32).astype(jnp.int16)
-            total = jnp.maximum(total, 1e-30)
-            sstat[i, h : h + 1, :] = top + jnp.log(total)
-            sstat[i, HEADS + h : HEADS + h + 1, :] = reach / (STEPS * total)
+            whole = jnp.round(accum * (STEPS / reach)).astype(jnp.int32)
+            lse = top + jnp.log(total)
+            scale = reach / (STEPS * total)
+            for n in range(2):
+                h = 2 * pair + n
+                lanes = slice(n * HALF, (n + 1) * HALF)
+                sbuf[half, i, h * WIDTH : (h + 1) * WIDTH, :] = whole[:, lanes].astype(jnp.int16)
+                sstat[half, i, h : h + 1, :] = lse[:, lanes]
+                sstat[half, i, HEADS + h : HEADS + h + 1, :] = scale[:, lanes]
 
         for t in range(HEADS + 2):
             if t < HEADS:
@@ -257,44 +279,46 @@
             if 0 <= t - 2 < HEADS:
                 phase_values(t - 2)
 
-        at_home = diagonal & (i == r)
-
-        @pl.when(at_home)
-        def _():
-            pltpu.make_async_copy(sbuf.at[i], rbuf.at[m], home_ls).start()
-            pltpu.make_async_copy(sstat.at[i], rstat.at[m], stat_ls).start()
-
-        @pl.when(jnp.logical_not(at_home))
-        def _():
-            remote(sbuf.at[i], rbuf.at[m], home_ss.at[i], home_rs.at[m], (i, r * 2 + e)).start()
-            remote(sstat.at[i], rstat.at[m], stat_ss.at[i], stat_rs.at[m], (i, r * 2 + e)).start()
+        for i in rows_i:
+            at_home = diagonal & (i == r)
+
+            @pl.when(at_home)
+            def _():
+                pltpu.make_async_copy(sbuf.at[half, i], rbuf.at[half, m], home_ls.at[half]).start()
+                pltpu.make_async_copy(sstat.at[half, i], rstat.at[half, m], stat_ls.at[half]).start()
+
+            @pl.when(jnp.logical_not(at_home))
+            def _():
+                remote(sbuf.at[half, i], rbuf.at[half, m], home_ss.at[half, i], home_rs.at[half, m], (i, r * 2 + e)).start()
+                remote(sstat.at[half, i], rstat.at[half, m], stat_ss.at[half, i], stat_rs.at[half, m], (i, r * 2 + e)).start()
 
         return carry
 
-    lax.fori_loop(0, NR, step, 0)
+    for half in range(2):
+        lax.fori_loop(0, NR // 2, functools.partial(step, half), 0)
 
     gatesT = contract(wgT[...], own[...], 1, 1).astype(BF16).astype(F32)
     gates = 1.0 / (1.0 + jnp.exp(-gatesT))
     loads[3].wait()
 
-    def home_arrived(k):
+    def home_arrived(half, k):
         is_self = diagonal & (m == k)
 
         @pl.when(is_self)
         def _():
-            pltpu.make_async_copy(sbuf.at[k], rbuf.at[k], home_ls).wait()
-            pltpu.make_async_copy(sstat.at[k], rstat.at[k], stat_ls).wait()
+            pltpu.make_async_copy(sbuf.at[half, k], rbuf.at[half, k], home_ls.at[half]).wait()
+            pltpu.make_async_copy(sstat.at[half, k], rstat.at[half, k], stat_ls.at[half]).wait()
 
         @pl.when(jnp.logical_not(is_self))
         def _():
-            remote(sbuf.at[k], rbuf.at[k], home_ss.at[k], home_rs.at[k], sib_dev).wait_recv()
-            remote(sstat.at[k], rstat.at[k], stat_ss.at[k], stat_rs.at[k], sib_dev).wait_recv()
-
-    def merge(group, so_far):
+            remote(sbuf.at[half, k], rbuf.at[half, k], home_ss.at[half, k], home_rs.at[half, k], sib_dev).wait_recv()
+            remote(sstat.at[half, k], rstat.at[half, k], stat_ss.at[half, k], stat_rs.at[half, k], sib_dev).wait_recv()
+
+    def merge(half, group, so_far):
         out = []
         for h in range(HEADS):
             low = h * WIDTH
-            tops = [rstat[k, h : h + 1, :] for k in group]
+            tops = [rstat[half, k, h : h + 1, :] for k in group]
             if so_far is not None:
                 tops.append(so_far[h][0])
             top = functools.reduce(jnp.maximum, tops)
@@ -303,7 +327,7 @@
             if so_far is not None:
                 total = total + factors[-1] * so_far[h][1]
             accum = sum(
-                (f * rstat[k, HEADS + h : HEADS + h + 1, :]) * rbuf[k, low : low + WIDTH, :].astype(jnp.int32).astype(F32)
+                (f * rstat[half, k, HEADS + h : HEADS + h + 1, :]) * rbuf[half, k, low : low + WIDTH, :].astype(jnp.int32).astype(F32)
                 for k, f in zip(group, factors)
             )
             if so_far is not None:
@@ -312,19 +336,20 @@
         return out
 
     senders = [((r // NYH - a + NZ) % NZ) * NYH + (r + b) % NYH for b in range(NYH) for a in range(NZ)]
-    for k in senders[:6]:
-        home_arrived(k)
-    early = merge(senders[:6], None)
-    for h in range(HEADS):
-        merged[h * WIDTH : (h + 1) * WIDTH, :] = early[h][2]
-    for k in senders[6:]:
-        home_arrived(k)
-    gated = [
-        (gates[h * WIDTH : (h + 1) * WIDTH] * (accum / total)).astype(BF16)
-        for h, (top, total, accum) in enumerate(merge(senders[6:], early))
-    ]
-    gatedT = jnp.concatenate(gated, axis=0)
-    out_ref[0] = contract(gatedT, w_out_ref[...], 0, 0).astype(BF16)
+    for half in range(2):
+        for k in senders[:6]:
+            home_arrived(half, k)
+        begun = merge(half, senders[:6], None)
+        for h in range(HEADS):
+            merged[h * WIDTH : (h + 1) * WIDTH, :] = begun[h][2]
+        for k in senders[6:]:
+            home_arrived(half, k)
+        gated = [
+            (gates[h * WIDTH : (h + 1) * WIDTH, half * HALF : (half + 1) * HALF] * (accum / total)).astype(BF16)
+            for h, (top, total, accum) in enumerate(merge(half, senders[6:], begun))
+        ]
+        gatedT = jnp.concatenate(gated, axis=0)
+        out_ref[0, half * HALF : (half + 1) * HALF, :] = contract(gatedT, w_out_ref[...], 0, 0).astype(BF16)
 
     for send in kv_sends + kv_ons + q_sends + q_ons:
         send.wait_send()
@@ -340,8 +365,9 @@
 
         @pl.when(jnp.logical_not(diagonal & (m == k)))
         def _():
-            remote(sbuf.at[k], rbuf.at[k], home_ss.at[k], home_rs.at[k], sib_dev).wait_send()
-            remote(sstat.at[k], rstat.at[k], stat_ss.at[k], stat_rs.at[k], sib_dev).wait_send()
+            for half in range(2):
+                remote(sbuf.at[half, k], rbuf.at[half, k], home_ss.at[half, k], home_rs.at[half, k], sib_dev).wait_send()
+                remote(sstat.at[half, k], rstat.at[half, k], stat_ss.at[half, k], stat_rs.at[half, k], sib_dev).wait_send()
 
 
 def local(pair_window, ln_gain, w_proj, w_out, pair_bias, chain_starts, chain_pads, residue_mask):
@@ -362,21 +388,23 @@
             pltpu.VMEM((LENGTH // KEYBLK, KEYBLK), jnp.int32),
             pltpu.VMEM((NR, 2, CHUNK, CH), BF16),
             pltpu.VMEM((NR, CHUNK, CH), BF16),
+            pltpu.VMEM((NR, KEYS, CH), BF16),
+            pltpu.VMEM((NR, CH, KEYS), BF16),
             pltpu.VMEM((2, HEADS, CHUNK, CHUNK), BF16),
-            pltpu.VMEM((HEADS, KEYS, CHUNK), F32),
+            pltpu.VMEM((2, HEADS // 2, KEYS, CHUNK), F32),
             pltpu.VMEM((CHUNK, CH), BF16),
             pltpu.VMEM((CH, CH), BF16),
             pltpu.VMEM((CH, CH), BF16),
             pltpu.VMEM((CH, CH), BF16),
             pltpu.VMEM((HEADS, KEYS, CHUNK), F32),
             pltpu.VMEM((HEADS, KEYS, CHUNK), BF16),
-            pltpu.VMEM((NR, CH, CHUNK), jnp.int16),
-            pltpu.VMEM((NR, STATS, CHUNK), F32),
-            pltpu.VMEM((NM, CH, CHUNK), jnp.int16),
-            pltpu.VMEM((NM, STATS, CHUNK), F32),
-            pltpu.VMEM((CH, CHUNK), F32),
+            pltpu.VMEM((2, NR, CH, HALF), jnp.int16),
+            pltpu.VMEM((2, NR, STATS, HALF), F32),
+            pltpu.VMEM((2, NM, CH, HALF), jnp.int16),
+            pltpu.VMEM((2, NM, STATS, HALF), F32),
+            pltpu.VMEM((CH, HALF), F32),
             dma((5,)), dma((7,)), dma((NR,)), dma((NR,)), dma((NR,)), dma((2, 7)), dma((2, NR)), dma((2,)), dma, dma, dma,
-            dma((NR,)), dma((NM,)), dma, dma((NR,)), dma((NM,)), dma,
+            dma((2, NR)), dma((2, NM)), dma((2,)), dma((2, NR)), dma((2, NM)), dma((2,)),
         ],
         compiler_params=pltpu.CompilerParams(
             collective_id=0, has_side_effects=True, vmem_limit_bytes=60 * 2**20

time: 38.7 us -> 37 us (0.956); the launches traced: 38 us -> 36.9 us
  Pallas kernels: 37.3 us -> 36.3 us
    pallas_call x1, Pallas kernels: 37.3 us -> 36.3 us  [local(): pl.pallas_call(kernel, out_shape=pltpu.VMEM((1, CHUNK, CH), BF16), in_spe...]
where the time goes in v5:
time: 37 us; the launch traced here: 36.9 us
  Pallas kernels  36.3 us (98%)
  local copies, waits for them, and re-layouts  0.63 us (2%)
    pallas_call x1, Pallas kernels, local(): pl.pallas_call(kernel, out_shape=pltpu.VMEM((1, CHUNK, CH), BF16), in_spe...  36.3 us

profile of v5, /device:TPU:0, one launch (start us, length us, event | category | flops | bytes accessed | tf_op | source)
XLA Modules:
  0.0 36.9 jit_solution(7226017354816964118)
XLA Ops:
  0.0 36.3 %triangle.1 = bf16[1,256,128]{2,1,0:T(8,128)(2,1)S(1)} custom-call(s32[4]{0:T(128)} %starts_ref.1, s32[4]{0:T(128)} %pads_ref.1, bf16[1,256,128]{2,1,0:T(8,128)(2,1)} %x_hbm.1, f32[1,128]{1,0:T(1,128)} %bitcast.3, bf16[128,512]{1,0:T(8,128)(2,1)} %w_hbm.1, bf16[128,128]{1,0:T(8,128)(2,1)} %w_out_hbm.1, s32[32,128]{1,0:T(8,128)} %bitcast.2, ...), custom_call_target="tpu_custom_call" | custom-call | tf_op jit(solution)/shard_map/triangle/pallas_call | solution.py:378
  36.3 0.6 %copy.10 = bf16[1,256,128]{2,1,0:T(8,128)(2,1)} copy(bf16[1,256,128]{2,1,0:T(8,128)(2,1)S(1)} %triangle.1) | data formatting | bytes 131072

commit v6 on v5

--- a/solution.py
+++ b/solution.py
@@ -167,8 +167,7 @@
         v = qbuf.at[i, halves[n]]
         return remote(v, v, q_ss.at[n, slot], q_rs.at[n, i], device)
 
-    q_sends = []
-    for n in range(2):
+    def share(n):
         @pl.when(jnp.logical_not(diagonal))
         def _():
             q_arrived(m, n)
@@ -176,9 +175,12 @@
         now = [q_copy(m, n, 0, key_dev(0, 1))] + [q_copy(m, n, a, key_dev(a, 0)) for a in (1, 3, 2)]
         for send in now:
             send.start()
-        q_sends += now
+        return now
+
+    first = share(0)
     bias_send.wait_recv()
     turn_bias(1 - e)
+    second = share(1)
     for a, b in ((1, 0), (3, 0), (2, 0), (1, 1), (3, 1), (2, 1)):
         to_sibling(row_at(a, b))
 
@@ -242,7 +244,7 @@
             for b in range(NBLK):
                 k0 = b * KEYBLK
                 weights = jnp.exp(s_scr[unit, k0 : k0 + KEYBLK, :] - tops[unit][b])
-                sums[unit].append(jnp.sum(weights, axis=0, keepdims=True))
+                sums[unit].append(jnp.sum(weights.reshape(KEYBLK // 8, 8, CHUNK), axis=0))
                 p_scr[unit, k0 : k0 + KEYBLK, :] = weights.astype(BF16)
 
         def phase_values(unit):
@@ -258,7 +260,7 @@
                 accs.append(jnp.concatenate([both[:WIDTH, :HALF], both[WIDTH:, HALF:]], axis=1))
             top = functools.reduce(jnp.maximum, tops[unit])
             factors = [jnp.exp(v - top) for v in tops[unit]]
-            total = jnp.maximum(sum(f * v for f, v in zip(factors, sums[unit])), 1e-30)
+            total = jnp.maximum(jnp.sum(sum(f * v for f, v in zip(factors, sums[unit])), axis=0, keepdims=True), 1e-30)
             accum = sum(f * v for f, v in zip(factors, accs))
             reach = jnp.maximum(jnp.max(jnp.abs(accum), axis=0, keepdims=True), 1e-30)
             whole = jnp.round(accum * (STEPS / reach)).astype(jnp.int32)
@@ -271,13 +273,18 @@
                 sstat[half, i, h : h + 1, :] = lse[:, lanes]
                 sstat[half, i, HEADS + h : HEADS + h + 1, :] = scale[:, lanes]
 
-        for t in range(HEADS + 2):
-            if t < HEADS:
-                phase_scores(t)
-            if 0 <= t - 1 < HEADS:
-                phase_weights(t - 1)
-            if 0 <= t - 2 < HEADS:
-                phase_values(t - 2)
+        phase_scores(0)
+        phase_scores(1)
+        phase_weights(0)
+        phase_scores(2)
+        phase_weights(1)
+        phase_values(0)
+        phase_scores(3)
+        phase_weights(2)
+        phase_values(1)
+        phase_weights(3)
+        phase_values(2)
+        phase_values(3)
 
         for i in rows_i:
             at_home = diagonal & (i == r)
@@ -351,7 +358,7 @@
         gatedT = jnp.concatenate(gated, axis=0)
         out_ref[0, half * HALF : (half + 1) * HALF, :] = contract(gatedT, w_out_ref[...], 0, 0).astype(BF16)
 
-    for send in kv_sends + kv_ons + q_sends + q_ons:
+    for send in kv_sends + kv_ons + first + second + q_ons:
         send.wait_send()
     bias_send.wait_send()
 

time: 37 us -> 36.6 us (0.989)
  Pallas kernels: 36.3 us -> 35.8 us
    pallas_call x1, Pallas kernels: 36.3 us -> 35.8 us  [local(): pl.pallas_call(kernel, out_shape=pltpu.VMEM((1, CHUNK, CH), BF16), in_spe...]
where the time goes in v6:
time: 36.6 us; the launch traced here: 36.4 us
  Pallas kernels  35.8 us (98%)
  local copies, waits for them, and re-layouts  0.63 us (2%)
    pallas_call x1, Pallas kernels, local(): pl.pallas_call(kernel, out_shape=pltpu.VMEM((1, CHUNK, CH), BF16), in_spe...  35.8 us

profile of v6, /device:TPU:0, one launch (start us, length us, event | category | flops | bytes accessed | tf_op | source)
XLA Modules:
  0.0 36.4 jit_solution(1982720752893270529)
XLA Ops:
  0.0 35.8 %triangle.1 = bf16[1,256,128]{2,1,0:T(8,128)(2,1)S(1)} custom-call(s32[4]{0:T(128)} %starts_ref.1, s32[4]{0:T(128)} %pads_ref.1, bf16[1,256,128]{2,1,0:T(8,128)(2,1)} %x_hbm.1, f32[1,128]{1,0:T(1,128)} %bitcast.3, bf16[128,512]{1,0:T(8,128)(2,1)} %w_hbm.1, bf16[128,128]{1,0:T(8,128)(2,1)} %w_out_hbm.1, s32[32,128]{1,0:T(8,128)} %bitcast.2, ...), custom_call_target="tpu_custom_call" | custom-call | tf_op jit(solution)/shard_map/triangle/pallas_call | solution.py:385
  35.8 0.6 %copy.10 = bf16[1,256,128]{2,1,0:T(8,128)(2,1)} copy(bf16[1,256,128]{2,1,0:T(8,128)(2,1)S(1)} %triangle.1) | data formatting | bytes 131072

commit v7 on v6

--- a/solution.py
+++ b/solution.py
@@ -33,6 +33,9 @@
 
 def contract(a, b, dim_a, dim_b):
     return lax.dot_general(a, b, (((dim_a,), (dim_b,)), ((), ())), preferred_element_type=F32)
+
+
+OTHERS = ((2, 1), (1, 1), (3, 1), (2, 0), (0, 1), (1, 0), (3, 0))
 
 
 def kernel(
@@ -71,14 +74,18 @@
     local_bias = pltpu.make_async_copy(bias_ref.at[:, pl.ds(pl.multiple_of(e * CHUNK, CHUNK), CHUNK), :], braw.at[e], bias_ls)
 
     barrier = pltpu.get_barrier_semaphore()
-    pl.semaphore_signal(barrier, inc=1, device_id=sib_dev, device_id_type=MESH)
-    for a, b in ((1, 0), (2, 0), (3, 0), (0, 1)):
-        pl.semaphore_signal(barrier, inc=1, device_id=row_dev(a, b), device_id_type=MESH)
-        pl.semaphore_signal(barrier, inc=1, device_id=key_dev(a, b), device_id_type=MESH)
-    for k in range(NM):
-        @pl.when(jnp.logical_not(diagonal & (m == k)))
-        def _():
-            pl.semaphore_signal(barrier, inc=1, device_id=(m, k * 2 + e), device_id_type=MESH)
+    def greet(device):
+        pl.semaphore_signal(barrier, inc=1, device_id=device, device_id_type=MESH)
+
+    greet(sib_dev)
+
+    @pl.when(jnp.logical_not(diagonal))
+    def _():
+        greet((m, r * 2 + e))
+
+    for a, b in OTHERS:
+        greet(row_dev(a, b))
+        greet(key_dev(a, b))
 
     for load in loads[2:] + [local_bias]:
         load.start()
@@ -93,7 +100,7 @@
     own[...] = normed
     nbuf[r, e] = normed
 
-    pl.semaphore_wait(barrier, 9 + jnp.where(diagonal, NR - 1, NR))
+    pl.semaphore_wait(barrier, 15 + jnp.where(diagonal, 0, 1))
 
     halves = [pl.ds(n * HALF, HALF) for n in range(2)]
     t_sends = [remote(own.at[v], qbuf.at[r, v], t_ss.at[n], q_rs.at[n, r], (m, r * 2 + e)) for n, v in enumerate(halves)]
@@ -296,8 +303,8 @@
 
             @pl.when(jnp.logical_not(at_home))
             def _():
+                remote(sstat.at[half, i], rstat.at[half, m], stat_ss.at[half, i], stat_rs.at[half, m], (i, r * 2 + e)).start()
                 remote(sbuf.at[half, i], rbuf.at[half, m], home_ss.at[half, i], home_rs.at[half, m], (i, r * 2 + e)).start()
-                remote(sstat.at[half, i], rstat.at[half, m], stat_ss.at[half, i], stat_rs.at[half, m], (i, r * 2 + e)).start()
 
         return carry
 

time: 36.6 us -> 36.7 us (level)
  no operation moved by 1% of the time
where the time goes in v7:
time: 36.7 us; the launch traced here: 36.5 us
  Pallas kernels  35.9 us (98%)
  local copies, waits for them, and re-layouts  0.63 us (2%)
    pallas_call x1, Pallas kernels, local(): pl.pallas_call(kernel, out_shape=pltpu.VMEM((1, CHUNK, CH), BF16), in_spe...  35.9 us

profile of v7, /device:TPU:0, one launch (start us, length us, event | category | flops | bytes accessed | tf_op | source)
XLA Modules:
  0.0 36.5 jit_solution(4650776982366953889)
XLA Ops:
  0.0 35.9 %triangle.1 = bf16[1,256,128]{2,1,0:T(8,128)(2,1)S(1)} custom-call(s32[4]{0:T(128)} %starts_ref.1, s32[4]{0:T(128)} %pads_ref.1, bf16[1,256,128]{2,1,0:T(8,128)(2,1)} %x_hbm.1, f32[1,128]{1,0:T(1,128)} %bitcast.3, bf16[128,512]{1,0:T(8,128)(2,1)} %w_hbm.1, bf16[128,128]{1,0:T(8,128)(2,1)} %w_out_hbm.1, s32[32,128]{1,0:T(8,128)} %bitcast.2, ...), custom_call_target="tpu_custom_call" | custom-call | tf_op jit(solution)/shard_map/triangle/pallas_call | solution.py:392
  35.9 0.6 %copy.10 = bf16[1,256,128]{2,1,0:T(8,128)(2,1)} copy(bf16[1,256,128]{2,1,0:T(8,128)(2,1)S(1)} %triangle.1) | data formatting | bytes 131072

commit v8 on v7

--- a/solution.py
+++ b/solution.py
@@ -19,7 +19,7 @@
 NM = NZ * NYH
 NCHAIN = 4
 LENGTH = 4096
-STATS = 2 * HEADS
+STATS = 3 * HEADS
 HALF = CHUNK // 2
 STEPS = 32767.0
 MESH = pl.DeviceIdType.MESH
@@ -267,18 +267,17 @@
                 accs.append(jnp.concatenate([both[:WIDTH, :HALF], both[WIDTH:, HALF:]], axis=1))
             top = functools.reduce(jnp.maximum, tops[unit])
             factors = [jnp.exp(v - top) for v in tops[unit]]
-            total = jnp.maximum(jnp.sum(sum(f * v for f, v in zip(factors, sums[unit])), axis=0, keepdims=True), 1e-30)
+            total = jnp.sum(sum(f * v for f, v in zip(factors, sums[unit])), axis=0, keepdims=True)
             accum = sum(f * v for f, v in zip(factors, accs))
             reach = jnp.maximum(jnp.max(jnp.abs(accum), axis=0, keepdims=True), 1e-30)
             whole = jnp.round(accum * (STEPS / reach)).astype(jnp.int32)
-            lse = top + jnp.log(total)
-            scale = reach / (STEPS * total)
+            scale = reach * (1.0 / STEPS)
             for n in range(2):
                 h = 2 * pair + n
                 lanes = slice(n * HALF, (n + 1) * HALF)
                 sbuf[half, i, h * WIDTH : (h + 1) * WIDTH, :] = whole[:, lanes].astype(jnp.int16)
-                sstat[half, i, h : h + 1, :] = lse[:, lanes]
-                sstat[half, i, HEADS + h : HEADS + h + 1, :] = scale[:, lanes]
+                for row, value in enumerate((top, total, scale)):
+                    sstat[half, i, row * HEADS + h : row * HEADS + h + 1, :] = value[:, lanes]
 
         phase_scores(0)
         phase_scores(1)
@@ -337,11 +336,11 @@
                 tops.append(so_far[h][0])
             top = functools.reduce(jnp.maximum, tops)
             factors = [jnp.exp(v - top) for v in tops]
-            total = sum(factors[: len(group)])
+            total = sum(f * rstat[half, k, HEADS + h : HEADS + h + 1, :] for k, f in zip(group, factors))
             if so_far is not None:
                 total = total + factors[-1] * so_far[h][1]
             accum = sum(
-                (f * rstat[half, k, HEADS + h : HEADS + h + 1, :]) * rbuf[half, k, low : low + WIDTH, :].astype(jnp.int32).astype(F32)
+                (f * rstat[half, k, 2 * HEADS + h : 2 * HEADS + h + 1, :]) * rbuf[half, k, low : low + WIDTH, :].astype(jnp.int32).astype(F32)
                 for k, f in zip(group, factors)
             )
             if so_far is not None:

time: 36.7 us -> 36.8 us (level)
  no operation moved by 1% of the time
where the time goes in v8:
time: 36.8 us; the launch traced here: 36.6 us
  Pallas kernels  36 us (98%)
  local copies, waits for them, and re-layouts  0.63 us (2%)
    pallas_call x1, Pallas kernels, local(): pl.pallas_call(kernel, out_shape=pltpu.VMEM((1, CHUNK, CH), BF16), in_spe...  36 us

profile of v8, /device:TPU:0, one launch (start us, length us, event | category | flops | bytes accessed | tf_op | source)
XLA Modules:
  0.0 36.6 jit_solution(11856466434294341148)
XLA Ops:
  0.0 36.0 %triangle.1 = bf16[1,256,128]{2,1,0:T(8,128)(2,1)S(1)} custom-call(s32[4]{0:T(128)} %starts_ref.1, s32[4]{0:T(128)} %pads_ref.1, bf16[1,256,128]{2,1,0:T(8,128)(2,1)} %x_hbm.1, f32[1,128]{1,0:T(1,128)} %bitcast.3, bf16[128,512]{1,0:T(8,128)(2,1)} %w_hbm.1, bf16[128,128]{1,0:T(8,128)(2,1)} %w_out_hbm.1, s32[32,128]{1,0:T(8,128)} %bitcast.2, ...), custom_call_target="tpu_custom_call" | custom-call | tf_op jit(solution)/shard_map/triangle/pallas_call | solution.py:391
  36.0 0.6 %copy.10 = bf16[1,256,128]{2,1,0:T(8,128)(2,1)} copy(bf16[1,256,128]{2,1,0:T(8,128)(2,1)S(1)} %triangle.1) | data formatting | bytes 131072
